TPU v7x, 32 devices: a whole 2x2x4 slice. The times are simulated.
32 devices in a mesh: gx: 8 (over y, x, core), gy: 4 (over z).
Axes of the slice: x: 2, y: 2, z: 4, core: 2. Of those that a mesh axis runs over, the one named last changes fastest.
Arguments:
- fv_state: float32 [4, 64, 64, 1024], P(None, 'gx', 'gy'), may hold values from -6 to 6
- buffer_owner: int32 [32768, 1], P(('gx', 'gy')), may hold values from 0 to 31; in each aligned block of 1024 rows (0 to 1023, 1024 to 2047, ...) at most 64 rows name the same one
- buffer_cell: int32 [32768], P(('gx', 'gy')), may hold values from 0 to 131071
- buffer_frac: float32 [3, 32768], P(None, ('gx', 'gy')), may hold values from 0 to 1
- buffer_count: int32 [32], P(('gx', 'gy')), may hold values from 341 to 1024, as said below
- sph_offset: float32 [3, 32, 16, 128], P(None, 'gx', 'gy'), may hold values from 0 to 1
- sph_vel: float32 [3, 32, 16, 128], P(None, 'gx', 'gy'), may hold values from -6 to 6
- sph_press: float32 [32, 16, 128], P('gx', 'gy'), may hold values from 0.1 to 1
- tile_count: int32 [32, 16], P('gx', 'gy'), may hold values from 64 to 128
Outputs:
- fv_next: float32 [4, 64, 64, 1024], P(None, 'gx', 'gy')
- buffer_state: float32 [4, 32768], P(None, ('gx', 'gy'))
- sph_accel: float32 [3, 32, 16, 128], P(None, 'gx', 'gy')
Inputs may be any that keep to these rules, and one draw needn't show every extreme that they name: `buffer_owner`: among the 1024 rows of one device, no owner is named by more than 64 rows, a bound that some block reaches. `buffer_count`: the live buffer slots of a device are its first ones; some device has 1024 live slots and some has 341. `tile_count`: the live particles of a tile occupy its first slots.
All inputs are finite; a program needn't handle non-finite values.
Results may differ from a plain program's by a relative error of at most 0.0003.
Values sent between devices are 32-bit elements; how exact they have to be, the bound alone decides.
A program may use at most 256 MiB of HBM per device.

v0:
```python
import jax
import jax.numpy as jnp
from jax import lax
from jax.sharding import PartitionSpec as P

STEP_RATIO = 0.3
VISCOSITY = 0.02
FORCE_SCALE = 0.1


def padded_2(array, sides, width):
    for axis, dim in sides:
        count, length = (lax.axis_size(axis), array.shape[dim])
        up = [(i, (i + 1) % count) for i in range(count - 1)]
        down = [(j, i) for i, j in up]
        last = lax.slice_in_dim(array, length - width, length, axis=dim)
        leading = lax.slice_in_dim(array, 0, width, axis=dim)
        before = lax.ppermute(last, axis, up)
        after = lax.ppermute(leading, axis, down)
        array = jnp.concatenate([before, array, after], axis=dim)
    return array


def from_behind(array, axis, by):
    count = lax.axis_size(axis)
    pairs = [(i, i + by) for i in range(count) if 0 <= i + by < count]
    return lax.ppermute(array, axis, pairs)


def face_flux(left_side, right_side, normal):
    jump_term = right_side - left_side
    fluxes = [-0.5 * jump_term[channel] for channel in range(4)]
    fluxes[0] = fluxes[0] + 0.5 * (left_side[normal] + right_side[normal])
    fluxes[normal] = fluxes[normal] + 0.5 * (left_side[0] + right_side[0])
    return jnp.stack(fluxes)


def flux_step(padded):
    interior = padded[:, 1:-1, 1:-1, 1:-1]
    slab_rows = padded[:, :, 1:-1, 1:-1]
    across = face_flux(slab_rows[:, :-1], slab_rows[:, 1:], 1)
    change = across[:, 1:] - across[:, :-1]
    slab_rows = padded[:, 1:-1, :, 1:-1]
    across = face_flux(slab_rows[:, :, :-1], slab_rows[:, :, 1:], 2)
    change = change + (across[:, :, 1:] - across[:, :, :-1])
    slab_rows = padded[:, 1:-1, 1:-1, :]
    across = face_flux(slab_rows[:, :, :, :-1], slab_rows[:, :, :, 1:], 3)
    change = change + (across[:, :, :, 1:] - across[:, :, :, :-1])
    return interior - STEP_RATIO * change


def answer_requests(upper, arrived):
    extent_x = upper.shape[1]
    extent_y = upper.shape[2]
    cells_y = extent_y - 1
    cells_z = upper.shape[3] - 1
    paired = jnp.concatenate([upper[:, :, :, :-1], upper[:, :, :, 1:]], axis=0)
    table = paired.reshape(8, extent_x * extent_y * cells_z).T
    cell_index = arrived[3].astype(jnp.int32)
    base_x = cell_index // (cells_y * cells_z)
    base_y = cell_index // cells_z % cells_y
    base_z = cell_index % cells_z
    frac_z = arrived[2][:, None]
    values = jnp.zeros((cell_index.shape[0], 4), jnp.float32)
    for corner in range(4):
        step_x = corner // 2
        step_y = corner % 2
        factor_x = arrived[0] if step_x else 1.0 - arrived[0]
        factor_y = arrived[1] if step_y else 1.0 - arrived[1]
        position = ((base_x + step_x) * extent_y + base_y + step_y) * cells_z + base_z
        fetched = jnp.take(table, position, axis=0)
        mixed = fetched[:, :4] * (1.0 - frac_z) + fetched[:, 4:] * frac_z
        values = values + (factor_x * factor_y)[:, None] * mixed
    return values.T


def pair_accel(own_tiles, other_tiles, shift_x, shift_y):
    separation_x = own_tiles[0][:, :, None] - other_tiles[0][:, None, :] - shift_x
    separation_y = own_tiles[1][:, :, None] - other_tiles[1][:, None, :] - shift_y
    separation_z = own_tiles[2][:, :, None] - other_tiles[2][:, None, :]
    distance = jnp.sqrt(
        separation_x * separation_x + separation_y * separation_y + separation_z * separation_z
    )
    closeness = jnp.maximum(1.0 - distance, 0.0)
    weight = 20.0 * closeness * closeness * closeness * other_tiles[7][:, None, :]
    push_term = (own_tiles[6][:, :, None] + other_tiles[6][:, None, :]) * weight
    weight_total = jnp.sum(weight, axis=-1)
    result = []
    for channel, separation in enumerate((separation_x, separation_y, separation_z)):
        drag_term = (
            jnp.sum(weight * other_tiles[3 + channel][:, None, :], axis=-1)
            - weight_total * own_tiles[3 + channel]
        )
        result.append(jnp.sum(push_term * separation, axis=-1) + VISCOSITY * drag_term)
    return jnp.stack(result)


def per_device(
    fv_state,
    buffer_owner,
    buffer_cell,
    buffer_frac,
    buffer_count,
    sph_offset,
    sph_vel,
    sph_press,
    tile_count,
):
    grid_x = lax.axis_size("gx")
    grid_y = lax.axis_size("gy")
    z_margin = ((0, 0), (0, 0), (0, 0), (1, 1))
    bordered = padded_2(fv_state, (("gx", 1), ("gy", 2)), 1)
    fv_next = flux_step(jnp.pad(bordered, z_margin))
    next_rows = from_behind(fv_next[:, :1], "gx", -1)
    widened_rows = jnp.concatenate([fv_next, next_rows], axis=1)
    next_columns = from_behind(widened_rows[:, :, :1], "gy", -1)
    upper = jnp.concatenate([widened_rows, next_columns], axis=2)
    upper = jnp.pad(upper, ((0, 0), (0, 0), (0, 0), (0, 1)))
    devices = grid_x * grid_y
    buffer_rows = buffer_cell.shape[0]
    capacity = 2 * buffer_rows // devices
    slot_total = devices * capacity
    owner_ids = buffer_owner[:, 0]
    row_ids = jnp.arange(buffer_rows, dtype=jnp.int32)
    is_live = row_ids < buffer_count[0]
    one_hot = (owner_ids[:, None] == jnp.arange(devices, dtype=jnp.int32)[None, :]) & is_live[
        :, None
    ]
    one_hot_float = one_hot.astype(jnp.bfloat16)
    lower_mask = (row_ids[None, :] < row_ids[:, None]).astype(jnp.bfloat16)
    earlier = jnp.dot(lower_mask, one_hot_float, preferred_element_type=jnp.float32)
    ranks = jnp.sum(jnp.where(one_hot, earlier, 0.0), axis=1).astype(jnp.int32)
    target = jnp.where(is_live, owner_ids * capacity + ranks, slot_total)
    selector = (target[:, None] == jnp.arange(slot_total, dtype=jnp.int32)[None, :]).astype(
        jnp.float32
    )
    request = jnp.concatenate([buffer_frac, buffer_cell[None].astype(jnp.float32)], axis=0)
    outgoing = jnp.dot(
        request, selector, precision=lax.Precision.HIGHEST, preferred_element_type=jnp.float32
    )
    arrived = lax.all_to_all(outgoing, ("gx", "gy"), split_axis=1, concat_axis=1, tiled=True)
    returned = lax.all_to_all(
        answer_requests(upper, arrived), ("gx", "gy"), split_axis=1, concat_axis=1, tiled=True
    )
    picked = lax.dot_general(
        returned,
        selector,
        (((1,), (1,)), ((), ())),
        precision=lax.Precision.HIGHEST,
        preferred_element_type=jnp.float32,
    )
    buffer_state = jnp.where(is_live[None, :], picked, 0.0)
    tiles_x, tiles_y, tile_slots = sph_press.shape
    tile_live = (
        jnp.arange(tile_slots, dtype=jnp.int32)[None, None, :] < tile_count[:, :, None]
    ).astype(jnp.float32)
    packed = jnp.concatenate([sph_offset, sph_vel, sph_press[None], tile_live[None]], axis=0)
    framed = padded_2(packed, (("gx", 1), ("gy", 2)), 1)
    own_tiles = packed.reshape(8, tiles_x * tiles_y, tile_slots)
    total = jnp.zeros((3, tiles_x * tiles_y, tile_slots), jnp.float32)
    for corner in range(9):
        step_x = corner // 3 - 1
        step_y = corner % 3 - 1
        other_tiles = framed[
            :, 1 + step_x : 1 + step_x + tiles_x, 1 + step_y : 1 + step_y + tiles_y
        ].reshape(8, tiles_x * tiles_y, tile_slots)
        total = total + pair_accel(own_tiles, other_tiles, float(step_x), float(step_y))
    sph_accel = (FORCE_SCALE * total * own_tiles[7][None]).reshape(3, tiles_x, tiles_y, tile_slots)
    return (fv_next, buffer_state, sph_accel)


def solution(mesh):
    return jax.shard_map(
        per_device,
        mesh=mesh,
        in_specs=(
            P(None, "gx", "gy", None),
            P(("gx", "gy"), None),
            P(("gx", "gy")),
            P(None, ("gx", "gy")),
            P(("gx", "gy")),
            P(None, "gx", "gy", None),
            P(None, "gx", "gy", None),
            P("gx", "gy", None),
            P("gx", "gy"),
        ),
        out_specs=(P(None, "gx", "gy", None), P(None, ("gx", "gy")), P(None, "gx", "gy", None)),
        check_vma=False,
    )
```

profile of v0, /device:TPU:1, one launch (start us, length us, event | category | flops | bytes accessed | tf_op | source)
XLA Modules:
  0.0 489.9 jit_solution(15305318396810796473)
XLA Ops:
  3.7 4.5 collective-permute-start.1
  16.5 5.6 %all-to-all-start = ((f32[32,1,256]{2,1,0:T(1,128)}), f32[32,1,256]{2,1,0:T(1,128)S(1)}, u32[]{:S(2)}, u32[]{:S(2)}) async-start(f32[32,1,256]{2,1,0:T(1,128)} %reshape.903), calls=%async_computation | async-start | bytes 65536 | tf_op jit(solution)/shard_map/all_to_all | solution.py:141
  27.8 4.4 constant_dynamic-update-slice_fusion
  37.6 3.5 multiply_reduce_fusion.32
  41.2 3.5 multiply_reduce_fusion.7
  45.0 3.6 multiply_reduce_fusion.3
  49.2 3.5 multiply_reduce_fusion.12
  53.4 3.5 multiply_reduce_fusion.17
  57.5 5.8 %multiply_reduce_fusion.20 = (f32[16,128]{1,0:T(8,128)S(1)}, f32[16,128]{1,0:T(8,128)S(1)}, f32[16,128]{1,0:T(8,128)S(1)}, f32[16,128]{1,0:T(8,128)S(1)}, f32[16...) fusion(f32[16,128]{1,0:T(8,128)S(1)} %bitcast.203, ...), kind=kLoop, calls=%fused_computation.194 | loop fusion | flops 15699968 | bytes 245760 | tf_op jit(solution)/shard_map/reduce_sum | solution.py:91
  64.0 3.5 multiply_reduce_fusion.24
  68.1 3.5 multiply_reduce_fusion.28
  77.6 4.8 collective-permute-start.3
  82.5 6.1 %dynamic-update-slice.1 = f32[4,9,16,1024]{3,1,2,0:T(8,128)} dynamic-update-slice(f32[4,9,16,1024]{3,1,2,0:T(8,128)} %get-tuple-element.141, f32[4,1,16,1024]{3,1,2,0:T(1,128)S(1)} %copy.65, s32[]{} %constant.152, s32[]{} %constant.153, s32[]{} %constant.152, s32[]{} %constant.152) | dynamic-update-slice | bytes 524292 | tf_op jit(solution)/shard_map/concatenate | solution.py:20
  93.7 4.2 select_maximum_fusion
  109.9 4.6 collective-permute-done.4
  116.7 5.2 %collective-permute-done.5 = f32[4,9,1,1024]{3,1,2,0:T(8,128)S(1)} collective-permute-done((f32[4,9,1,1024]{3,1,2,0:T(8,128)S(1)}, f32[4,9,1,1024]{3,1,2,0:T(8,128)S(1)}, u32[]{:S(2)}, u32[]{:S(2)}) %collective-permute-start.5) | collective-permute-done | bytes 147488 | tf_op jit(solution)/shard_map/ppermute | solution.py:27
  123.1 4.1 pad_maximum_fusion
  127.2 39.0 %copy.75 = f32[8,9,17,1024]{0,3,2,1:T(8,128)} copy(f32[8,9,17,1024]{3,1,2,0:T(8,128)} %pad_maximum_fusion) | data formatting | bytes 10027008 | tf_op jit(solution)/shard_map/concatenate | solution.py:57
  166.2 73.8 %gather_fusion.3 = f32[2048,8]{1,0:T(8,128)S(1)} fusion(f32[156672,8]{1,0:T(8,128)} %bitcast.6, s32[2048]{0:T(1024)S(1)} %copy-done.16), kind=kCustom, calls=%fused_computation.3.clone | custom fusion | bytes 139264 | tf_op jit(solution)/shard_map/jit(_take)/gather | solution.py:71
  240.3 73.5 %gather_fusion.2 = f32[2048,8]{1,0:T(8,128)S(1)} fusion(f32[156672,8]{1,0:T(8,128)} %bitcast.6, s32[2048]{0:T(1024)S(1)} %copy-done.15), kind=kCustom, calls=%fused_computation.2.clone | custom fusion | bytes 139264 | tf_op jit(solution)/shard_map/jit(_take)/gather | solution.py:71
  314.1 74.3 %gather_fusion.1 = f32[2048,8]{1,0:T(8,128)S(1)} fusion(f32[156672,8]{1,0:T(8,128)} %bitcast.6, s32[2048]{0:T(1024)S(1)} %copy-done.14), kind=kCustom, calls=%fused_computation.1.clone | custom fusion | bytes 139264 | tf_op jit(solution)/shard_map/jit(_take)/gather | solution.py:71
  388.8 74.2 %gather_fusion = f32[2048,8]{1,0:T(8,128)S(1)} fusion(f32[156672,8]{1,0:T(8,128)} %bitcast.6, s32[2048]{0:T(1024)S(1)} %copy-done.13), kind=kCustom, calls=%fused_computation.clone | custom fusion | bytes 139264 | tf_op jit(solution)/shard_map/jit(_take)/gather | solution.py:71
  466.4 11.1 %all-to-all-start.1 = ((f32[32,1,256]{2,1,0:T(1,128)}), f32[32,1,256]{2,1,0:T(1,128)S(1)}, u32[]{:S(2)}, u32[]{:S(2)}) async-start(f32[32,1,256]{2,1,0:T(1,128)} %reshape.905), calls=%async_computation.1 | async-start | bytes 65536 | tf_op jit(solution)/shard_map/all_to_all | solution.py:142
  485.2 4.5 fusion.15
  (145 shorter events, 63.3 us)
Async XLA Ops:
  1.8 73.2 %collective-permute-start = (f32[4,1,16,1024]{3,2,1,0:T(8,128)S(1)}, f32[4,1,16,1024]{3,2,1,0:T(8,128)S(1)}, u32[]{:S(2)}, u32[]{:S(2)}) collective-permute-start(f32[4,1,16,1024]{3,2,1,0:T(8,128)S(1)} %get-tuple-element.144), channel_id=1, source_target_pairs={{4,0},{8,4},{12,8},{16,12},{20,16},{24,20},{28,24},{5,1},{9,5},{13... | collective-permute-start | bytes 786440 | tf_op jit(solution)/shard_map/ppermute | solution.py:19
  3.7 71.5 %collective-permute-start.1 = (f32[4,1,16,1024]{3,2,1,0:T(8,128)S(1)}, f32[4,1,16,1024]{3,2,1,0:T(8,128)S(1)}, u32[]{:S(2)}, u32[]{:S(2)}) collective-permute-start(f32[4,1,16,1024]{3,2,1,0:T(8,128)S(1)} %get-tuple-element.143), channel_id=1, source_target_pairs={{0,4},{4,8},{8,12},{12,16},{16,20},{20,24},{24,28},{1,5},{5,9},{9,... | collective-permute-start | bytes 786440 | tf_op jit(solution)/shard_map/ppermute | solution.py:18
  16.5 56.4 %all-to-all-start = ((f32[32,1,256]{2,1,0:T(1,128)}), f32[32,1,256]{2,1,0:T(1,128)S(1)}, u32[]{:S(2)}, u32[]{:S(2)}) async-start(f32[32,1,256]{2,1,0:T(1,128)} %reshape.903), calls=%async_computation | async-start | bytes 65536 | tf_op jit(solution)/shard_map/all_to_all | solution.py:141
  22.2 10.2 %collective-permute-start.7 = (f32[8,1,4,128]{3,2,1,0:T(4,128)S(1)}, f32[8,1,4,128]{3,2,1,0:T(4,128)S(1)}, u32[]{:S(2)}, u32[]{:S(2)}) collective-permute-start(f32[8,1,4,128]{3,2,1,0:T(4,128)S(1)} %get-tuple-element.214), channel_id=1, source_target_pairs={{4,0},{8,4},{12,8},{16,12},{20,16},{24,20},{28,24},{5,1},{9,5},{13... | collective-permute-start | bytes 49160 | tf_op jit(solution)/shard_map/ppermute | solution.py:19
  24.4 8.0 %collective-permute-start.6 = (f32[8,1,4,128]{3,2,1,0:T(4,128)S(1)}, f32[8,1,4,128]{3,2,1,0:T(4,128)S(1)}, u32[]{:S(2)}, u32[]{:S(2)}) collective-permute-start(f32[8,1,4,128]{3,2,1,0:T(4,128)S(1)} %get-tuple-element.213), channel_id=1, source_target_pairs={{0,4},{4,8},{8,12},{12,16},{16,20},{20,24},{24,28},{1,5},{5,9},{9,... | collective-permute-start | bytes 49160 | tf_op jit(solution)/shard_map/ppermute | solution.py:18
  32.5 12.3 %collective-permute-start.8 = (f32[8,6,1,128]{3,2,1,0:T(1,128)S(1)}, f32[8,6,1,128]{3,2,1,0:T(1,128)S(1)}, u32[]{:S(2)}, u32[]{:S(2)}) collective-permute-start(f32[8,6,1,128]{3,2,1,0:T(1,128)S(1)} %get-tuple-element.195), channel_id=1, source_target_pairs={{0,1},{1,2},{2,3},{4,5},{5,6},{6,7},{8,9},{9,10},{10,11},{12,13},{... | collective-permute-start | bytes 73736 | tf_op jit(solution)/shard_map/ppermute | solution.py:18
  35.8 9.0 %collective-permute-start.9 = (f32[8,6,1,128]{3,2,1,0:T(1,128)S(1)}, f32[8,6,1,128]{3,2,1,0:T(1,128)S(1)}, u32[]{:S(2)}, u32[]{:S(2)}) collective-permute-start(f32[8,6,1,128]{3,2,1,0:T(1,128)S(1)} %get-tuple-element.196), channel_id=1, source_target_pairs={{1,0},{2,1},{3,2},{5,4},{6,5},{7,6},{9,8},{10,9},{11,10},{13,12},{... | collective-permute-start | bytes 73736 | tf_op jit(solution)/shard_map/ppermute | solution.py:19
  76.4 17.3 %collective-permute-start.2 = (f32[4,10,1,1024]{3,1,2,0:T(8,128)}, f32[4,10,1,1024]{3,1,2,0:T(8,128)S(1)}, u32[]{:S(2)}, u32[]{:S(2)}) collective-permute-start(f32[4,10,1,1024]{3,1,2,0:T(8,128)} %get-tuple-element.137), channel_id=1, source_target_pairs={{1,0},{2,1},{3,2},{5,4},{6,5},{7,6},{9,8},{10,9},{11,10},{13,12},{... | collective-permute-start | bytes 491528 | tf_op jit(solution)/shard_map/ppermute | solution.py:19
  77.6 16.1 %collective-permute-start.3 = (f32[4,10,1,1024]{3,1,2,0:T(8,128)S(1)}, f32[4,10,1,1024]{3,1,2,0:T(8,128)S(1)}, u32[]{:S(2)}, u32[]{:S(2)}) collective-permute-start(f32[4,10,1,1024]{3,1,2,0:T(8,128)S(1)} %get-tuple-element.136), channel_id=1, source_target_pairs={{0,1},{1,2},{2,3},{4,5},{5,6},{6,7},{8,9},{9,10},{10,11},{12,13},{... | collective-permute-start | bytes 491528 | tf_op jit(solution)/shard_map/ppermute | solution.py:18
  106.8 7.7 %collective-permute-start.4 = (f32[4,1,16,1024]{3,2,1,0:T(8,128)S(1)}, f32[4,1,16,1024]{3,2,1,0:T(8,128)S(1)}, u32[]{:S(2)}, u32[]{:S(2)}) collective-permute-start(f32[4,1,16,1024]{3,2,1,0:T(8,128)S(1)} %copy.73), channel_id=1, source_target_pairs={{4,0},{8,4},{12,8},{16,12},{20,16},{24,20},{28,24},{5,1},{9,5},{13... | collective-permute-start | bytes 786440 | tf_op jit(solution)/shard_map/ppermute | solution.py:27
  114.8 7.1 %collective-permute-start.5 = (f32[4,9,1,1024]{3,1,2,0:T(8,128)S(1)}, f32[4,9,1,1024]{3,1,2,0:T(8,128)S(1)}, u32[]{:S(2)}, u32[]{:S(2)}) collective-permute-start(f32[4,9,1,1024]{3,1,2,0:T(8,128)S(1)} %pad_maximum_fusion.6), channel_id=1, source_target_pairs={{1,0},{2,1},{3,2},{5,4},{6,5},{7,6},{9,8},{10,9},{11,10},{13,12},{... | collective-permute-start | bytes 442376 | tf_op jit(solution)/shard_map/ppermute | solution.py:27
  127.2 39.0 %copy-start.16 = (s32[2048]{0:T(1024)S(1)}, s32[2048]{0:T(1024)}, u32[]{:S(2)}) copy-start(s32[2048]{0:T(1024)} %get-tuple-element.257) | copy-start | bytes 24580
  166.2 74.1 %copy-start.15 = (s32[2048]{0:T(1024)S(1)}, s32[2048]{0:T(1024)}, u32[]{:S(2)}) copy-start(s32[2048]{0:T(1024)} %get-tuple-element.259) | copy-start | bytes 24580
  240.3 73.8 %copy-start.14 = (s32[2048]{0:T(1024)S(1)}, s32[2048]{0:T(1024)}, u32[]{:S(2)}) copy-start(s32[2048]{0:T(1024)} %get-tuple-element.258) | copy-start | bytes 24580
  314.1 74.6 %copy-start.13 = (s32[2048]{0:T(1024)S(1)}, s32[2048]{0:T(1024)}, u32[]{:S(2)}) copy-start(s32[2048]{0:T(1024)} %get-tuple-element.256) | copy-start | bytes 24580
  388.7 88.9 %copy-start.5 = (f32[1,4,4,128]{3,2,1,0:T(4,128)S(1)}, f32[1,4,4,128]{3,2,1,0:T(4,128)}, u32[]{:S(2)}) copy-start(f32[1,4,4,128]{3,2,1,0:T(4,128)} %get-tuple-element.241) | copy-start | bytes 24580
  388.7 88.9 %copy-start.6 = (f32[1,4,4,128]{3,2,1,0:T(4,128)S(1)}, f32[1,4,4,128]{3,2,1,0:T(4,128)}, u32[]{:S(2)}) copy-start(f32[1,4,4,128]{3,2,1,0:T(4,128)} %get-tuple-element.233) | copy-start | bytes 24580
  388.7 88.9 %copy-start.7 = (f32[1,4,4,128]{3,2,1,0:T(4,128)S(1)}, f32[1,4,4,128]{3,2,1,0:T(4,128)}, u32[]{:S(2)}) copy-start(f32[1,4,4,128]{3,2,1,0:T(4,128)} %get-tuple-element.234) | copy-start | bytes 24580
  388.7 88.9 %copy-start.8 = (f32[1,4,4,128]{3,2,1,0:T(4,128)S(1)}, f32[1,4,4,128]{3,2,1,0:T(4,128)}, u32[]{:S(2)}) copy-start(f32[1,4,4,128]{3,2,1,0:T(4,128)} %get-tuple-element.235) | copy-start | bytes 24580
  388.8 88.9 %copy-start.9 = (f32[1,4,4,128]{3,2,1,0:T(4,128)S(1)}, f32[1,4,4,128]{3,2,1,0:T(4,128)}, u32[]{:S(2)}) copy-start(f32[1,4,4,128]{3,2,1,0:T(4,128)} %get-tuple-element.230) | copy-start | bytes 24580
  388.8 88.9 %copy-start.10 = (f32[1,4,4,128]{3,2,1,0:T(4,128)S(1)}, f32[1,4,4,128]{3,2,1,0:T(4,128)}, u32[]{:S(2)}) copy-start(f32[1,4,4,128]{3,2,1,0:T(4,128)} %get-tuple-element.231) | copy-start | bytes 24580
  388.8 88.9 %copy-start.11 = (f32[1,4,4,128]{3,2,1,0:T(4,128)S(1)}, f32[1,4,4,128]{3,2,1,0:T(4,128)}, u32[]{:S(2)}) copy-start(f32[1,4,4,128]{3,2,1,0:T(4,128)} %get-tuple-element.232) | copy-start | bytes 24580
  388.8 88.9 %copy-start.12 = (f32[1,4,4,128]{3,2,1,0:T(4,128)S(1)}, f32[1,4,4,128]{3,2,1,0:T(4,128)}, u32[]{:S(2)}) copy-start(f32[1,4,4,128]{3,2,1,0:T(4,128)} %get-tuple-element.227) | copy-start | bytes 24580
  466.4 17.9 %all-to-all-start.1 = ((f32[32,1,256]{2,1,0:T(1,128)}), f32[32,1,256]{2,1,0:T(1,128)S(1)}, u32[]{:S(2)}, u32[]{:S(2)}) async-start(f32[32,1,256]{2,1,0:T(1,128)} %reshape.905), calls=%async_computation.1 | async-start | bytes 65536 | tf_op jit(solution)/shard_map/all_to_all | solution.py:142
  (10 other events, 140.0 us)
where the time goes:
time: 497 us; the launch traced here: 490 us
  local copies, waits for them, and re-layouts  356 us (72%)
  other arithmetic  66.7 us (13%)
  starting transfers between devices  43.3 us (9%)
  waiting for transfers between devices  12.4 us (2%)
  matrix products  9.23 us (2%)
    gather x8, local copies, waits for them, and re-layouts, answer_requests(): fetched = jnp.take(table, position, axis=0)  297 us
    concatenate x1, local copies, waits for them, and re-layouts, answer_requests(): paired = jnp.concatenate([upper[:, :, :, :-1], upper[:, :, :, 1:]], axis=0)  39 us
    reduce_sum x8, other arithmetic, pair_accel(): jnp.sum(weight * other_tiles[3 + channel][:, None, :], axis=-1)  30.5 us
    ppermute x4, starting transfers between devices, padded_2(): before = lax.ppermute(last, axis, up)  16 us
    all_to_all x1, starting transfers between devices, per_device(): lax.all_to_all(answer_requests(upper, arrived), ('gx', 'gy'), split_axis=...  11.1 us
    unnamed x50, local copies, waits for them, and re-layouts  10.3 us
  transfers between devices with their start and end apart: 12, of which 3 were waited for; matrix products, arithmetic and copies ran while one was open for 13% of the time, Pallas kernels for 0%

commit v1 on v0

v1 whole, which is shorter than its diff:
```python
import functools

import jax
import jax.numpy as jnp
from jax import lax
from jax.experimental import pallas as pl
from jax.experimental.pallas import tpu as pltpu
from jax.sharding import PartitionSpec as P

STEP_RATIO = 0.3
VISCOSITY = 0.02
FORCE_SCALE = 0.1
LANES = 128
F32 = jnp.float32
BF16 = jnp.bfloat16


def split(value):
    high = value.astype(BF16)
    return high, (value - high.astype(F32)).astype(BF16)


def dot(left, right):
    return jnp.dot(left, right, preferred_element_type=F32)


def sweep(centre, left, right, down, up):
    length = centre.shape[-1]
    lane = lax.broadcasted_iota(jnp.int32, centre.shape[1:], 1)
    below, above = [], []
    for c in range(4):
        below.append(jnp.where(lane == 0, 0.0, pltpu.roll(centre[c], 1, 1)))
        above.append(jnp.where(lane == length - 1, 0.0, pltpu.roll(centre[c], length - 1, 1)))
    lean = [
        (right[1] - left[1]) + (up[2] - down[2]) + (above[3] - below[3]),
        right[0] - left[0],
        up[0] - down[0],
        above[0] - below[0],
    ]
    result = []
    for c in range(4):
        around = (left[c] + right[c]) + (down[c] + up[c]) + (below[c] + above[c])
        result.append(
            (1.0 - 3.0 * STEP_RATIO) * centre[c] + (0.5 * STEP_RATIO) * (around - lean[c])
        )
    return result


def sweep_block(slabs, y_low, y_up, y_up2, y_top, fv_out, high, low, keep_x, keep_y):
    cells_x, cells_y = fv_out.shape[1], fv_out.shape[2]
    length = fv_out.shape[3]
    row = lax.broadcasted_iota(jnp.int32, (cells_y, length), 0)

    def slab(x, keep):
        centre = slabs[:, x + 1]
        first = y_low[:, pl.ds(x + 1, 1), :]
        last = y_up[:, pl.ds(x + 1, 1), :]
        down = [jnp.where(row == 0, first[c], pltpu.roll(centre[c], 1, 0)) for c in range(4)]
        up = [
            jnp.where(row == cells_y - 1, last[c], pltpu.roll(centre[c], cells_y - 1, 0))
            for c in range(4)
        ]
        new = sweep(centre, slabs[:, x], slabs[:, x + 2], down, up)
        y_top[:, pl.ds(x, 1), :] = centre[:, cells_y - 1 :, :]
        for c in range(4):
            value = new[c] if keep is None else new[c] * keep
            if keep is None:
                fv_out[c, x] = value
            high[c, pl.ds(x * cells_y, cells_y), :], low[c, pl.ds(x * cells_y, cells_y), :] = split(
                value
            )

    def step(x, carry):
        slab(x, None)
        return carry

    lax.fori_loop(0, cells_x, step, 0)
    slab(cells_x, keep_x)
    rows = 16
    y_top[:, cells_x + 1 :, :] = jnp.zeros((4, rows - cells_x - 1, length), F32)
    new = sweep(
        y_up[:, 1 : 1 + rows],
        y_up[:, 0:rows],
        y_up[:, 2 : 2 + rows],
        y_top[...],
        y_up2[:, 1 : 1 + rows],
    )
    edge = lax.broadcasted_iota(jnp.int32, (rows, length), 0)
    factor = jnp.where(edge < cells_x, keep_y, jnp.where(edge == cells_x, keep_x * keep_y, 0.0))
    start = (cells_x + 1) * cells_y
    for c in range(4):
        high[c, start : start + rows, :], low[c, start : start + rows, :] = split(new[c] * factor)


def blend(index, fraction, count, base=0):
    spot = lax.broadcasted_iota(jnp.int32, (count, index.shape[1]), 0) + base
    return jnp.where(spot == index, 1.0 - fraction, jnp.where(spot == index + 1, fraction, 0.0))


def interpolate(asked, high, low, shape, put, width):
    _, cells_x, cells_y, length = shape
    rows = high.shape[1]

    def tile(t, carry):
        lanes = pl.ds(pl.multiple_of(t * width, width), width)
        cell = asked[3:4, lanes].astype(jnp.int32)
        k = cell % length
        plane = cell // length
        spot = lax.broadcasted_iota(jnp.int32, (length, width), 0)
        c = asked[2:3, lanes]
        w_high, w_low = split(blend(k, c, length))
        t_high = high[...].reshape(4 * rows, length)
        t_low = low[...].reshape(4 * rows, length)
        mixed = dot(t_high, w_high) + dot(t_low, w_high) + dot(t_high, w_low)
        weight_y = blend(plane % cells_y, asked[1:2, lanes], cells_y)
        last_y = jnp.where(plane % cells_y == cells_y - 1, asked[1:2, lanes], 0.0)
        weight_x = blend(plane // cells_y, asked[0:1, lanes], 16)
        out = []
        for channel in range(4):
            first = channel * rows
            total = jnp.zeros((cells_y, width), F32)
            for x in range(cells_x + 1):
                part = mixed[first + x * cells_y : first + (x + 1) * cells_y]
                total = total + weight_x[x : x + 1] * part
            edge = mixed[first + rows - 16 : first + rows] * weight_x
            out.append(
                jnp.sum(total * weight_y, axis=0, keepdims=True)
                + last_y * jnp.sum(edge, axis=0, keepdims=True)
            )
        put(t, jnp.concatenate(out, axis=0))
        return carry

    lax.fori_loop(0, asked.shape[1] // width, tile, 0)


def route(owner, count, devices):
    rows = owner.shape[1]
    live = lax.broadcasted_iota(jnp.int32, (1, rows), 1) < count
    place = lax.broadcasted_iota(jnp.int32, (devices, rows), 0)
    named = jnp.where((place == owner) & live, 1.0, 0.0)
    blocks = rows // LANES
    stacked = jnp.concatenate(
        [named[:, b * LANES : (b + 1) * LANES] for b in range(blocks)], axis=0
    ).astype(BF16)
    source = lax.broadcasted_iota(jnp.int32, (LANES, 2 * LANES), 0)
    target = lax.broadcasted_iota(jnp.int32, (LANES, 2 * LANES), 1)
    ladder = jnp.where((source < target) | (target >= LANES), 1.0, 0.0).astype(BF16)
    tallies = dot(stacked, ladder)
    running = jnp.zeros((devices, LANES), F32)
    ranks = []
    for b in range(blocks):
        part = tallies[b * devices : (b + 1) * devices]
        earlier = part[:, :LANES] + running
        running = running + part[:, LANES:]
        ranks.append(
            jnp.sum(earlier * named[:, b * LANES : (b + 1) * LANES], axis=0, keepdims=True)
        )
    rank = jnp.concatenate(ranks, axis=1).astype(jnp.int32)
    slot = lax.broadcasted_iota(jnp.int32, (LANES, rows), 0)
    ranked = jnp.where((slot == rank) & live, 1.0, 0.0).astype(BF16)
    return named, ranked


def pack(named, ranked, frac, cell, put):
    devices = named.shape[0]
    fields = []
    for d in range(3):
        high = frac[d : d + 1].astype(BF16).astype(F32)
        fields += [high, frac[d : d + 1] - high]
    fields += [
        (cell // 65536).astype(F32),
        (cell // 256 % 256).astype(F32),
        (cell % 256).astype(F32),
    ]
    stacked = jnp.concatenate([(named * field).astype(BF16) for field in fields], axis=0)
    sent = lax.dot_general(
        stacked, ranked, (((1,), (1,)), ((), ())), preferred_element_type=F32
    )
    part = [sent[f * devices : (f + 1) * devices] for f in range(9)]
    put(0, part[0] + part[1])
    put(1, part[2] + part[3])
    put(2, part[4] + part[5])
    put(3, part[6] * 65536.0 + part[7] * 256.0 + part[8])


def pick(named, ranked, answers):
    devices = named.shape[0]
    high, low = split(answers)
    spread = dot(high, ranked) + dot(low, ranked)
    return jnp.concatenate(
        [
            jnp.sum(spread[c * devices : (c + 1) * devices] * named, axis=0, keepdims=True)
            for c in range(4)
        ],
        axis=0,
    )


def pair_forces(tiles, put, tiles_x, tiles_y):
    slots = tiles.shape[3]
    row = lax.broadcasted_iota(jnp.int32, (8, slots), 0)

    def one(index, carry):
        m = index // tiles_y
        n = index % tiles_y
        own = tiles[m + 1, n + 1]
        sums = jnp.zeros((16, slots), F32)
        for a in range(3):
            w_high, w_low, f_high, f_low = [], [], [], []
            for b in range(3):
                other = tiles[m + a, n + b]
                shift = jnp.where(row == 0, a - 1.0, jnp.where(row == 1, b - 1.0, 0.0))
                other = other + shift
                columns = jnp.transpose(other)
                e = [own[d : d + 1] - columns[:, d : d + 1] for d in range(3)]
                s = jnp.sqrt(e[0] * e[0] + e[1] * e[1] + e[2] * e[2])
                near = jnp.maximum(1.0 - s, 0.0)
                high, low = split(near * near * near)
                w_high.append(high)
                w_low.append(low)
                masked = other * other[7:8]
                high, low = split(jnp.concatenate([masked, masked * other[6:7]], axis=0))
                f_high.append(high)
                f_low.append(low)
            w_high, w_low = jnp.concatenate(w_high, axis=0), jnp.concatenate(w_low, axis=0)
            f_high, f_low = jnp.concatenate(f_high, axis=1), jnp.concatenate(f_low, axis=1)
            both = dot(jnp.concatenate([f_high, f_low], axis=0), w_high)
            sums = sums + both[:16] + both[16:] + dot(f_high, w_low)
        result = []
        for d in range(3):
            push = (
                own[6:7] * (own[d : d + 1] * sums[7:8] - sums[d : d + 1])
                + own[d : d + 1] * sums[6:7]
                - sums[8 + d : 9 + d]
            )
            drag = sums[3 + d : 4 + d] - own[3 + d : 4 + d] * sums[7:8]
            result.append((20.0 * FORCE_SCALE) * own[7:8] * (push + VISCOSITY * drag))
        put(m, n, result)
        return carry

    lax.fori_loop(0, tiles_x * tiles_y, one, 0)


def pack_kernel(devices, owner_ref, cell_ref, frac_ref, count_ref, out_ref):
    named, ranked = route(owner_ref[...], count_ref[0], devices)

    def put(f, value):
        out_ref[:, f, :] = value

    pack(named, ranked, frac_ref[...], cell_ref[...], put)


def pick_kernel(devices, owner_ref, count_ref, answer_ref, out_ref):
    named, ranked = route(owner_ref[...], count_ref[0], devices)
    answers = jnp.concatenate([answer_ref[:, c, :] for c in range(4)], axis=0)
    out_ref[...] = pick(named, ranked, answers)


def block_kernel(slabs, y_low, y_up, y_up2, asked, fv_out, answer, high, low, y_top):
    keep_x = jnp.where(lax.axis_index("gx") < lax.axis_size("gx") - 1, 1.0, 0.0)
    keep_y = jnp.where(lax.axis_index("gy") < lax.axis_size("gy") - 1, 1.0, 0.0)
    sweep_block(slabs, y_low, y_up, y_up2, y_top, fv_out, high, low, keep_x, keep_y)
    width = 512

    def put(t, value):
        answer[:, pl.ds(pl.multiple_of(t * width, width), width)] = value

    interpolate(asked, high, low, fv_out.shape, put, width)


def sph_kernel(tiles_ref, out_ref):
    tiles_x, tiles_y = out_ref.shape[1], out_ref.shape[2]

    def put(m, n, result):
        for d in range(3):
            out_ref[d, m, pl.ds(n, 1), :] = result[d]

    pair_forces(tiles_ref, put, tiles_x, tiles_y)


def shifted(array, axis, by):
    count = lax.axis_size(axis)
    return lax.ppermute(array, axis, [(i, i + by) for i in range(count) if 0 <= i + by < count])


PARAMS = pltpu.CompilerParams(vmem_limit_bytes=48 * 1024 * 1024)
SMEM = pl.BlockSpec(memory_space=pltpu.SMEM)
VMEM = pl.BlockSpec(memory_space=pltpu.VMEM)


def per_device(
    fv_state,
    buffer_owner,
    buffer_cell,
    buffer_frac,
    buffer_count,
    sph_offset,
    sph_vel,
    sph_press,
    tile_count,
):
    devices = lax.axis_size("gx") * lax.axis_size("gy")
    _, cells_x, cells_y, length = fv_state.shape
    rows = buffer_cell.shape[0]
    capacity = 2 * rows // devices
    owner = buffer_owner.reshape(1, rows)
    cell = buffer_cell.reshape(1, rows)
    outgoing = pl.pallas_call(
        functools.partial(pack_kernel, devices),
        out_shape=jax.ShapeDtypeStruct((devices, 4, LANES), F32),
        in_specs=[VMEM, VMEM, VMEM, SMEM],
        out_specs=VMEM,
        compiler_params=PARAMS,
    )(owner, cell, buffer_frac, buffer_count)
    arrived = lax.all_to_all(
        outgoing[:, :, :capacity], ("gx", "gy"), split_axis=0, concat_axis=0, tiled=True
    )
    asked = jnp.transpose(arrived, (1, 0, 2)).reshape(4, devices * capacity)
    before = shifted(fv_state[:, -1:], "gx", 1)
    after = shifted(fv_state[:, :2], "gx", -1)
    slabs = jnp.concatenate([before, fv_state, after], axis=1)
    y_low = shifted(slabs[:, :, -1], "gy", 1)
    y_up = shifted(slabs[:, :, :2], "gy", -1)
    pad = ((0, 0), (0, 18 - cells_x - 3), (0, 0))
    fv_next, answers = pl.pallas_call(
        block_kernel,
        out_shape=(
            jax.ShapeDtypeStruct(fv_state.shape, F32),
            jax.ShapeDtypeStruct((4, devices * capacity), F32),
        ),
        in_specs=[VMEM] * 5,
        out_specs=(VMEM, VMEM),
        scratch_shapes=[
            pltpu.VMEM((4, (cells_x + 1) * cells_y + 16, length), BF16),
            pltpu.VMEM((4, (cells_x + 1) * cells_y + 16, length), BF16),
            pltpu.VMEM((4, 16, length), F32),
        ],
        compiler_params=PARAMS,
    )(slabs, y_low, jnp.pad(y_up[:, :, 0], pad), jnp.pad(y_up[:, :, 1], pad), asked)
    returned = lax.all_to_all(
        jnp.transpose(answers.reshape(4, devices, capacity), (1, 0, 2)),
        ("gx", "gy"),
        split_axis=0,
        concat_axis=0,
        tiled=True,
    )
    buffer_state = pl.pallas_call(
        functools.partial(pick_kernel, devices),
        out_shape=jax.ShapeDtypeStruct((4, rows), F32),
        in_specs=[VMEM, SMEM, VMEM],
        out_specs=VMEM,
        compiler_params=PARAMS,
    )(owner, buffer_count, jnp.pad(returned, ((0, 0), (0, 0), (0, LANES - capacity))))
    slots = sph_press.shape[2]
    live = (jnp.arange(slots, dtype=jnp.int32) < tile_count[:, :, None]).astype(F32)
    packed = jnp.concatenate([sph_offset, sph_vel, sph_press[None], live[None]], axis=0)
    packed = jnp.transpose(packed, (1, 2, 0, 3))
    packed = jnp.concatenate(
        [shifted(packed[-1:], "gx", 1), packed, shifted(packed[:1], "gx", -1)], axis=0
    )
    packed = jnp.concatenate(
        [shifted(packed[:, -1:], "gy", 1), packed, shifted(packed[:, :1], "gy", -1)], axis=1
    )
    sph_accel = pl.pallas_call(
        sph_kernel,
        out_shape=jax.ShapeDtypeStruct(sph_offset.shape, F32),
        in_specs=[VMEM],
        out_specs=VMEM,
        compiler_params=PARAMS,
    )(packed)
    return fv_next, buffer_state, sph_accel


def solution(mesh):
    return jax.shard_map(
        per_device,
        mesh=mesh,
        in_specs=(
            P(None, "gx", "gy", None),
            P(("gx", "gy"), None),
            P(("gx", "gy")),
            P(None, ("gx", "gy")),
            P(("gx", "gy")),
            P(None, "gx", "gy", None),
            P(None, "gx", "gy", None),
            P("gx", "gy", None),
            P("gx", "gy"),
        ),
        out_specs=(P(None, "gx", "gy", None), P(None, ("gx", "gy")), P(None, "gx", "gy", None)),
        check_vma=False,
    )
```

time: 497 us -> 88.5 us (0.18); the launches traced: 490 us -> 87.7 us
  local copies, waits for them, and re-layouts: 356 us -> 10.7 us
  other arithmetic: 66.7 us -> 2.48 us
  Pallas kernels: 0 us -> 30.9 us
  starting transfers between devices: 43.3 us -> 33.9 us
  matrix products: 9.23 us -> 0 us
    gather x8 -> x0, local copies, waits for them, and re-layouts: 297 us -> none  [answer_requests(): fetched = jnp.take(table, position, axis=0)]
    concatenate x2 -> x1, local copies, waits for them, and re-layouts: 45.1 us -> 3.86 us  [per_device(): slabs = jnp.concatenate([before, fv_state, after], axis=1)]
    pallas_call x0 -> x4, Pallas kernels: none -> 30.9 us  [the longest x1 17.1 us: per_device(): pl.pallas_call(sph_kernel, out_shape=jax.ShapeDtypeStruct(sph_offset.shap...]
    reduce_sum x8 -> x0, other arithmetic: 30.5 us -> none  [pair_accel(): jnp.sum(weight * other_tiles[3 + channel][:, None, :], axis=-1)]
    concatenate x9 -> x2, other arithmetic: 12.1 us -> 0.91 us  [the longest x1 0.9 us: per_device(): slabs = jnp.concatenate([before, fv_state, after], axis=1)]
    dot_general x3 -> x0, matrix products: 9.23 us -> none  [the longest x1 4.46 us: per_device(): lax.dot_general(returned, selector, (((1,), (1,)), ((), ())), precision=l...]
    sub x4 -> x0, other arithmetic: 7.65 us -> none  [the longest x3 5.04 us: face_flux(): jump_term = right_side - left_side]
    add x12 -> x0, other arithmetic: 6.65 us -> none  [the longest x9 4.37 us: pair_accel(): jnp.sum(push_term * separation, axis=-1) + VISCOSITY * drag_term]
  transfers between devices with their start and end apart: 12 -> 10, of which waited for: 3 -> 3; matrix products, arithmetic and copies ran while one was open for 13% -> 11% of each run, Pallas kernels for 0% -> 34%
where the time goes in v1:
time: 88.5 us; the launch traced here: 87.7 us
  starting transfers between devices  33.9 us (38%)
  Pallas kernels  30.9 us (35%)
  local copies, waits for them, and re-layouts  10.7 us (12%)
  waiting for transfers between devices  7.99 us (9%)
  other arithmetic  2.48 us (3%)
  between operations  1.76 us (2%)
    ppermute x8, starting transfers between devices, shifted(): lax.ppermute(array, axis, [(i, i + by) for i in range(count) if 0 <= i +...  21 us
    pallas_call x1, Pallas kernels, per_device(): pl.pallas_call(sph_kernel, out_shape=jax.ShapeDtypeStruct(sph_offset.shap...  17.1 us
    pallas_call x1, Pallas kernels, per_device(): pl.pallas_call(block_kernel, out_shape=(jax.ShapeDtypeStruct(fv_state.sha...  12.1 us
    all_to_all x1, starting transfers between devices, per_device(): lax.all_to_all(outgoing[:, :, :capacity], ('gx', 'gy'), split_axis=0, con...  8 us
    ppermute x8, waiting for transfers between devices, shifted(): lax.ppermute(array, axis, [(i, i + by) for i in range(count) if 0 <= i +...  5.49 us
    all_to_all x1, starting transfers between devices, per_device(): lax.all_to_all(jnp.transpose(answers.reshape(4, devices, capacity), (1, 0...  4.97 us
    unnamed x23, local copies, waits for them, and re-layouts  4.53 us
    concatenate x1, local copies, waits for them, and re-layouts, per_device(): slabs = jnp.concatenate([before, fv_state, after], axis=1)  3.86 us
  transfers between devices with their start and end apart: 10, of which 3 were waited for; matrix products, arithmetic and copies ran while one was open for 11% of the time, Pallas kernels for 34%

profile of v1, /device:TPU:1, one launch (start us, length us, event | category | flops | bytes accessed | tf_op | source)
XLA Modules:
  0.0 87.7 jit_solution(1000550165008403604)
XLA Ops:
  0.7 2.8 %copy.21 = f32[4,8,16,1024]{3,1,0,2:T(8,128)S(1)} copy(f32[4,8,16,1024]{3,2,1,0:T(8,128)} %param.9) | data formatting | bytes 4194304 | tf_op args[0]
  3.7 2.0 %collective-permute-start.1 = (f32[4,2,16,1024]{3,1,0,2:T(2,128)S(1)}, f32[4,2,16,1024]{3,1,0,2:T(2,128)S(1)}, u32[]{:S(2)}, u32[]{:S(2)}) collective-permute-start(f32[4,2,16,1024]{3,1,0,2:T(2,128)S(1)} %slice.44), channel_id=1, source_target_pairs={{4,0},{8,4},{12,8},{16,12},{20,16},{24,20},{28,24},{5,1},{9,5},{13... | collective-permute-start | bytes 1572872 | tf_op jit(solution)/shard_map/ppermute | solution.py:283
  6.0 4.5 %collective-permute-start = (f32[4,1,16,1024]{3,1,0,2:T(1,128)S(1)}, f32[4,1,16,1024]{3,1,0,2:T(1,128)S(1)}, u32[]{:S(2)}, u32[]{:S(2)}) collective-permute-start(f32[4,1,16,1024]{3,1,0,2:T(1,128)S(1)} %copy.19), channel_id=1, source_target_pairs={{0,4},{4,8},{8,12},{12,16},{16,20},{20,24},{24,28},{1,5},{5,9},{9,... | collective-permute-start | bytes 786440 | tf_op jit(solution)/shard_map/ppermute | solution.py:283
  10.7 1.9 %collective-permute-start.5 = (f32[1,4,8,128]{3,2,1,0:T(8,128)S(1)}, f32[1,4,8,128]{3,2,1,0:T(8,128)S(1)}, u32[]{:S(2)}, u32[]{:S(2)}) collective-permute-start(f32[1,4,8,128]{3,2,1,0:T(8,128)S(1)} %get-tuple-element.12), channel_id=1, source_target_pairs={{4,0},{8,4},{12,8},{16,12},{20,16},{24,20},{28,24},{5,1},{9,5},{13... | collective-permute-start | bytes 49160 | tf_op jit(solution)/shard_map/ppermute | solution.py:283
  12.6 3.6 %collective-permute-start.4 = (f32[1,4,8,128]{3,2,1,0:T(8,128)S(1)}, f32[1,4,8,128]{3,2,1,0:T(8,128)S(1)}, u32[]{:S(2)}, u32[]{:S(2)}) collective-permute-start(f32[1,4,8,128]{3,2,1,0:T(8,128)S(1)} %get-tuple-element.11), channel_id=1, source_target_pairs={{0,4},{4,8},{8,12},{12,16},{16,20},{20,24},{24,28},{1,5},{5,9},{9,... | collective-permute-start | bytes 49160 | tf_op jit(solution)/shard_map/ppermute | solution.py:283
  16.6 0.9 %pad_maximum_fusion = f32[4,11,16,1024]{3,1,0,2:T(8,128)S(1)} fusion(f32[4,2,16,1024]{3,1,0,2:T(2,128)S(1)} %collective-permute-done.1, f32[4,8,16,1024]{3,1,0,2:T(8,128)S(1)} %copy.21, f32[4,1,16,1024]{3,1,0,2:T(1,128)S(1)} %collective-permute-done), kind=kLoop, calls=%fused_computation | loop fusion | flops 1441792 | bytes 5767168 | tf_op jit(solution)/shard_map/concatenate | solution.py:321
  17.6 1.3 %collective-permute-start.3 = (f32[4,11,2,1024]{3,1,0,2:T(8,128)S(1)}, f32[4,11,2,1024]{3,1,0,2:T(8,128)S(1)}, u32[]{:S(2)}, u32[]{:S(2)}) collective-permute-start(f32[4,11,2,1024]{3,1,0,2:T(8,128)S(1)} %slice.46), channel_id=1, source_target_pairs={{1,0},{2,1},{3,2},{5,4},{6,5},{7,6},{9,8},{10,9},{11,10},{13,12},{... | collective-permute-start | bytes 1081352 | tf_op jit(solution)/shard_map/ppermute | solution.py:283
  19.6 0.5 shard_map.112
  20.1 0.7 reshape.32
  20.9 8.0 %all-to-all-start = ((f32[32,1,256]{2,1,0:T(1,128)}), f32[32,1,256]{2,1,0:T(1,128)S(1)}, u32[]{:S(2)}, u32[]{:S(2)}) async-start(f32[32,1,256]{2,1,0:T(1,128)} %reshape.32), calls=%async_computation | async-start | bytes 65536 | tf_op jit(solution)/shard_map/all_to_all | solution.py:315
  28.9 1.3 %collective-permute-start.7 = (f32[6,1,8,128]{3,2,1,0:T(8,128)S(1)}, f32[6,1,8,128]{3,2,1,0:T(8,128)S(1)}, u32[]{:S(2)}, u32[]{:S(2)}) collective-permute-start(f32[6,1,8,128]{3,2,1,0:T(8,128)S(1)} %get-tuple-element.10), channel_id=1, source_target_pairs={{1,0},{2,1},{3,2},{5,4},{6,5},{7,6},{9,8},{10,9},{11,10},{13,12},{... | collective-permute-start | bytes 73736 | tf_op jit(solution)/shard_map/ppermute | solution.py:283
  30.2 4.0 %collective-permute-start.6 = (f32[6,1,8,128]{3,2,1,0:T(8,128)S(1)}, f32[6,1,8,128]{3,2,1,0:T(8,128)S(1)}, u32[]{:S(2)}, u32[]{:S(2)}) collective-permute-start(f32[6,1,8,128]{3,2,1,0:T(8,128)S(1)} %get-tuple-element.9), channel_id=1, source_target_pairs={{0,1},{1,2},{2,3},{4,5},{5,6},{6,7},{8,9},{9,10},{10,11},{12,13},{... | collective-permute-start | bytes 73736 | tf_op jit(solution)/shard_map/ppermute | solution.py:283
  34.2 2.5 %all-to-all-done = f32[32,1,256]{2,1,0:T(1,128)S(1)} async-done(((f32[32,1,256]{2,1,0:T(1,128)}), f32[32,1,256]{2,1,0:T(1,128)S(1)}, u32[]{:S(2)}, u32[]{:S(2)}) %all-to-all-start) | async-done | bytes 32800 | tf_op jit(solution)/shard_map/all_to_all | solution.py:315
  37.2 0.7 reduce
  38.1 3.9 %copy.23.slabs = f32[4,11,16,1024]{3,2,1,0:T(8,128)S(1)} copy(f32[4,11,16,1024]{3,1,0,2:T(8,128)} %copy-done.3) | data formatting | bytes 5767168 | tf_op jit(solution)/shard_map/concatenate | solution.py:321
  42.0 1.0 %slice_bitcast_fusion.2 = f32[4,11,1024]{2,1,0:T(8,128)S(1)} fusion(f32[4,11,16,1024]{3,1,0,2:T(8,128)} %copy-done.3), kind=kLoop, calls=%fused_computation.3 | loop fusion | bytes 360448 | tf_op jit(solution)/shard_map/squeeze | solution.py:322
  43.0 2.4 %collective-permute-start.2 = (f32[4,11,1024]{2,1,0:T(8,128)S(1)}, f32[4,11,1024]{2,1,0:T(8,128)S(1)}, u32[]{:S(2)}, u32[]{:S(2)}) collective-permute-start(f32[4,11,1024]{2,1,0:T(8,128)S(1)} %slice_bitcast_fusion.2), channel_id=1, source_target_pairs={{0,1},{1,2},{2,3},{4,5},{5,6},{6,7},{8,9},{9,10},{10,11},{12,13},{... | collective-permute-start | bytes 540680 | tf_op jit(solution)/shard_map/ppermute | solution.py:283
  45.5 5.1 %collective-permute-done.2.y_low = f32[4,11,1024]{2,1,0:T(8,128)S(1)} collective-permute-done((f32[4,11,1024]{2,1,0:T(8,128)S(1)}, f32[4,11,1024]{2,1,0:T(8,128)S(1)}, u32[]{:S(2)}, u32[]{:S(2)}) %collective-permute-start.2) | collective-permute-done | bytes 180256 | tf_op jit(solution)/shard_map/ppermute | solution.py:283
  50.7 12.1 %shard_map.113 = (f32[4,8,16,1024]{3,2,1,0:T(8,128)}, f32[4,2048]{1,0:T(4,128)S(1)}) custom-call(f32[4,11,16,1024]{3,2,1,0:T(8,128)S(1)} %copy.23.slabs, f32[4,11,1024]{2,1,0:T(8,128)S(1)} %collective-permute-done.2.y_low, f32[4,18,1024]{2,1,0:T(8,128)S(1)} %pad.11.y_up, f32[4,18,1024]{2,1,0:T(8,128)S(1)} %pad.12.y_up2, f32[4,2048]{1,0:T(4,128)S(1)} %reshape.30.asked), custom_call_target="tpu_custom_call" | custom-call | tf_op jit(solution)/shard_map/pallas_call | solution.py:325
  62.9 0.7 reshape.34
  63.6 5.0 %all-to-all-start.1 = ((f32[32,1,256]{2,1,0:T(1,128)}), f32[32,1,256]{2,1,0:T(1,128)S(1)}, u32[]{:S(2)}, u32[]{:S(2)}) async-start(f32[32,1,256]{2,1,0:T(1,128)} %reshape.34), calls=%async_computation.1 | async-start | bytes 65536 | tf_op jit(solution)/shard_map/all_to_all | solution.py:340
  68.6 17.1 %shard_map.115 = f32[3,4,4,128]{3,2,1,0:T(4,128)} custom-call(f32[6,6,8,128]{3,2,1,0:T(8,128)S(1)} %pad_maximum_fusion.1.tiles_ref), custom_call_target="tpu_custom_call" | custom-call | tf_op jit(solution)/shard_map/pallas_call | solution.py:364
  85.7 0.7 reduce.1
  86.6 1.1 %shard_map.114 = f32[4,1024]{1,0:T(4,128)} custom-call(s32[1,1024]{1,0:T(1,128)S(1)} %bitcast.18, s32[1]{0:T(128)S(6)} %copy.29.count_ref, f32[32,4,128]{2,1,0:T(4,128)S(1)} %pad.13.answer_ref), custom_call_target="tpu_custom_call" | custom-call | tf_op jit(solution)/shard_map/pallas_call | solution.py:347
  (47 shorter events, 2.1 us)
Async XLA Ops:
  0.6 5.0 %slice-start = ((f32[4,8,16,1024]{3,2,1,0:T(8,128)}), f32[4,1,16,1024]{3,2,1,0:T(8,128)S(1)}, s32[]{:S(2)}) async-start(f32[4,8,16,1024]{3,2,1,0:T(8,128)} %param.9), calls=%async_computation.2 | async-start | bytes 524288 | tf_op jit(solution)/shard_map/slice | solution.py:319
  0.6 9.8 %copy-start.4 = (f32[3,4,4,128]{3,2,1,0:T(4,128)S(1)}, f32[3,4,4,128]{3,2,1,0:T(4,128)}, u32[]{:S(2)}) copy-start(f32[3,4,4,128]{3,2,1,0:T(4,128)} %param.15) | copy-start | bytes 73732
  0.7 9.8 %copy-start.5 = (f32[3,4,4,128]{3,2,1,0:T(4,128)S(1)}, f32[3,4,4,128]{3,2,1,0:T(4,128)}, u32[]{:S(2)}) copy-start(f32[3,4,4,128]{3,2,1,0:T(4,128)} %param.14) | copy-start | bytes 73732
  0.7 9.8 %copy-start.7 = (s32[4,4]{1,0:T(4,128)S(1)}, s32[4,4]{1,0:T(4,128)}, u32[]{:S(2)}) copy-start(s32[4,4]{1,0:T(4,128)} %param.17) | copy-start | bytes 196
  0.7 10.0 %copy-start.6 = (f32[4,4,128]{2,1,0:T(4,128)S(1)}, f32[4,4,128]{2,1,0:T(4,128)}, u32[]{:S(2)}) copy-start(f32[4,4,128]{2,1,0:T(4,128)} %param.16) | copy-start | bytes 24580
  3.7 12.9 %collective-permute-start.1 = (f32[4,2,16,1024]{3,1,0,2:T(2,128)S(1)}, f32[4,2,16,1024]{3,1,0,2:T(2,128)S(1)}, u32[]{:S(2)}, u32[]{:S(2)}) collective-permute-start(f32[4,2,16,1024]{3,1,0,2:T(2,128)S(1)} %slice.44), channel_id=1, source_target_pairs={{4,0},{8,4},{12,8},{16,12},{20,16},{24,20},{28,24},{5,1},{9,5},{13... | collective-permute-start | bytes 1572872 | tf_op jit(solution)/shard_map/ppermute | solution.py:283
  6.0 10.3 %collective-permute-start = (f32[4,1,16,1024]{3,1,0,2:T(1,128)S(1)}, f32[4,1,16,1024]{3,1,0,2:T(1,128)S(1)}, u32[]{:S(2)}, u32[]{:S(2)}) collective-permute-start(f32[4,1,16,1024]{3,1,0,2:T(1,128)S(1)} %copy.19), channel_id=1, source_target_pairs={{0,4},{4,8},{8,12},{12,16},{16,20},{20,24},{24,28},{1,5},{5,9},{9,... | collective-permute-start | bytes 786440 | tf_op jit(solution)/shard_map/ppermute | solution.py:283
  10.5 9.1 %copy-start = (f32[3,1024]{1,0:T(4,128)S(1)}, f32[3,1024]{1,0:T(4,128)}, u32[]{:S(2)}) copy-start(f32[3,1024]{1,0:T(4,128)} %frac_ref.1) | copy-start | bytes 36868
  10.5 9.1 %copy-start.1 = (s32[1024,1]{0,1:T(1,128)S(1)}, s32[1024,1]{0,1:T(1,128)}, u32[]{:S(2)}) copy-start(s32[1024,1]{0,1:T(1,128)} %param.10) | copy-start | bytes 12292
  10.5 9.1 %copy-start.2 = (s32[1024]{0:T(1024)S(1)}, s32[1024]{0:T(1024)}, u32[]{:S(2)}) copy-start(s32[1024]{0:T(1024)} %param.11) | copy-start | bytes 12292
  10.7 18.2 %collective-permute-start.5 = (f32[1,4,8,128]{3,2,1,0:T(8,128)S(1)}, f32[1,4,8,128]{3,2,1,0:T(8,128)S(1)}, u32[]{:S(2)}, u32[]{:S(2)}) collective-permute-start(f32[1,4,8,128]{3,2,1,0:T(8,128)S(1)} %get-tuple-element.12), channel_id=1, source_target_pairs={{4,0},{8,4},{12,8},{16,12},{20,16},{24,20},{28,24},{5,1},{9,5},{13... | collective-permute-start | bytes 49160 | tf_op jit(solution)/shard_map/ppermute | solution.py:283
  12.6 16.3 %collective-permute-start.4 = (f32[1,4,8,128]{3,2,1,0:T(8,128)S(1)}, f32[1,4,8,128]{3,2,1,0:T(8,128)S(1)}, u32[]{:S(2)}, u32[]{:S(2)}) collective-permute-start(f32[1,4,8,128]{3,2,1,0:T(8,128)S(1)} %get-tuple-element.11), channel_id=1, source_target_pairs={{0,4},{4,8},{8,12},{12,16},{16,20},{20,24},{24,28},{1,5},{5,9},{9,... | collective-permute-start | bytes 49160 | tf_op jit(solution)/shard_map/ppermute | solution.py:283
  17.5 2.0 %copy-start.3 = (f32[4,11,16,1024]{3,1,0,2:T(8,128)}, f32[4,11,16,1024]{3,1,0,2:T(8,128)S(1)}, u32[]{:S(2)}) copy-start(f32[4,11,16,1024]{3,1,0,2:T(8,128)S(1)} %pad_maximum_fusion) | copy-start | bytes 8650756
  17.6 27.8 %collective-permute-start.3 = (f32[4,11,2,1024]{3,1,0,2:T(8,128)S(1)}, f32[4,11,2,1024]{3,1,0,2:T(8,128)S(1)}, u32[]{:S(2)}, u32[]{:S(2)}) collective-permute-start(f32[4,11,2,1024]{3,1,0,2:T(8,128)S(1)} %slice.46), channel_id=1, source_target_pairs={{1,0},{2,1},{3,2},{5,4},{6,5},{7,6},{9,8},{10,9},{11,10},{13,12},{... | collective-permute-start | bytes 1081352 | tf_op jit(solution)/shard_map/ppermute | solution.py:283
  20.9 15.8 %all-to-all-start = ((f32[32,1,256]{2,1,0:T(1,128)}), f32[32,1,256]{2,1,0:T(1,128)S(1)}, u32[]{:S(2)}, u32[]{:S(2)}) async-start(f32[32,1,256]{2,1,0:T(1,128)} %reshape.32), calls=%async_computation | async-start | bytes 65536 | tf_op jit(solution)/shard_map/all_to_all | solution.py:315
  28.9 39.7 %collective-permute-start.7 = (f32[6,1,8,128]{3,2,1,0:T(8,128)S(1)}, f32[6,1,8,128]{3,2,1,0:T(8,128)S(1)}, u32[]{:S(2)}, u32[]{:S(2)}) collective-permute-start(f32[6,1,8,128]{3,2,1,0:T(8,128)S(1)} %get-tuple-element.10), channel_id=1, source_target_pairs={{1,0},{2,1},{3,2},{5,4},{6,5},{7,6},{9,8},{10,9},{11,10},{13,12},{... | collective-permute-start | bytes 73736 | tf_op jit(solution)/shard_map/ppermute | solution.py:283
  30.2 38.4 %collective-permute-start.6 = (f32[6,1,8,128]{3,2,1,0:T(8,128)S(1)}, f32[6,1,8,128]{3,2,1,0:T(8,128)S(1)}, u32[]{:S(2)}, u32[]{:S(2)}) collective-permute-start(f32[6,1,8,128]{3,2,1,0:T(8,128)S(1)} %get-tuple-element.9), channel_id=1, source_target_pairs={{0,1},{1,2},{2,3},{4,5},{5,6},{6,7},{8,9},{9,10},{10,11},{12,13},{... | collective-permute-start | bytes 73736 | tf_op jit(solution)/shard_map/ppermute | solution.py:283
  43.0 7.7 %collective-permute-start.2 = (f32[4,11,1024]{2,1,0:T(8,128)S(1)}, f32[4,11,1024]{2,1,0:T(8,128)S(1)}, u32[]{:S(2)}, u32[]{:S(2)}) collective-permute-start(f32[4,11,1024]{2,1,0:T(8,128)S(1)} %slice_bitcast_fusion.2), channel_id=1, source_target_pairs={{0,1},{1,2},{2,3},{4,5},{5,6},{6,7},{8,9},{9,10},{10,11},{12,13},{... | collective-permute-start | bytes 540680 | tf_op jit(solution)/shard_map/ppermute | solution.py:283
  63.6 22.1 %all-to-all-start.1 = ((f32[32,1,256]{2,1,0:T(1,128)}), f32[32,1,256]{2,1,0:T(1,128)S(1)}, u32[]{:S(2)}, u32[]{:S(2)}) async-start(f32[32,1,256]{2,1,0:T(1,128)} %reshape.34), calls=%async_computation.1 | async-start | bytes 65536 | tf_op jit(solution)/shard_map/all_to_all | solution.py:340

commit v2 on v1

--- a/solution.py
+++ b/solution.py
@@ -196,13 +196,12 @@
     )
 
 
-def pair_forces(tiles, put, tiles_x, tiles_y):
+def pair_forces(tiles, put, count, place):
     slots = tiles.shape[3]
     row = lax.broadcasted_iota(jnp.int32, (8, slots), 0)
 
     def one(index, carry):
-        m = index // tiles_y
-        n = index % tiles_y
+        m, n = place(index)
         own = tiles[m + 1, n + 1]
         sums = jnp.zeros((16, slots), F32)
         for a in range(3):
@@ -238,54 +237,239 @@
         put(m, n, result)
         return carry
 
-    lax.fori_loop(0, tiles_x * tiles_y, one, 0)
-
-
-def pack_kernel(devices, owner_ref, cell_ref, frac_ref, count_ref, out_ref):
+    lax.fori_loop(0, count, one, 0)
+
+
+def whole_kernel(
+    grid,
+    capacity,
+    owner_ref,
+    cell_ref,
+    frac_ref,
+    count_ref,
+    fv,
+    packed,
+    fv_out,
+    state_out,
+    accel_out,
+    slabs,
+    fresh,
+    stage,
+    landed,
+    corner_out,
+    corner_in,
+    y_low,
+    y_up,
+    y_up2,
+    y_top,
+    high,
+    low,
+    tiles,
+    ask_out,
+    ask_in,
+    asked,
+    reply_out,
+    reply_in,
+    near_send,
+    near_recv,
+    ask_send,
+    ask_recv,
+    reply_send,
+    reply_recv,
+    local_sem,
+):
+    grid_x, grid_y = grid
+    devices = grid_x * grid_y
+    gx, gy = lax.axis_index("gx"), lax.axis_index("gy")
+    me = gx * grid_y + gy
+    _, cells_x, cells_y, length = fresh.shape
+    tiles_x, tiles_y = packed.shape[0], packed.shape[1]
+    load = pltpu.make_async_copy(fv, slabs.at[:, 1 : 1 + cells_x], local_sem.at[0])
+    load.start()
+
+    for ref in (landed, corner_in, y_low, y_up, y_up2):
+        ref[...] = jnp.zeros(ref.shape, ref.dtype)
+    for x in (0, cells_x + 1, cells_x + 2):
+        slabs[:, x] = jnp.zeros((4, cells_y, length), F32)
+    for n in range(tiles_y + 2):
+        tiles[0, n] = jnp.zeros(tiles.shape[2:], F32)
+        tiles[tiles_x + 1, n] = jnp.zeros(tiles.shape[2:], F32)
+    for m in range(tiles_x):
+        tiles[m + 1, 0] = jnp.zeros(tiles.shape[2:], F32)
+        tiles[m + 1, tiles_y + 1] = jnp.zeros(tiles.shape[2:], F32)
+        for n in range(tiles_y):
+            tiles[m + 1, n + 1] = packed[m, n]
+
+    def everyone(action):
+        def step(p, carry):
+            action(lax.rem(me + p, devices))
+            return carry
+
+        lax.fori_loop(1, devices, step, 0)
+
+    def at(device):
+        return {"gx": device // grid_y, "gy": lax.rem(device, grid_y)}
+
+    barrier = pltpu.get_barrier_semaphore()
+    everyone(
+        lambda other: pl.semaphore_signal(
+            barrier, inc=1, device_id=at(other), device_id_type=pl.DeviceIdType.MESH
+        )
+    )
+
     named, ranked = route(owner_ref[...], count_ref[0], devices)
 
-    def put(f, value):
-        out_ref[:, f, :] = value
-
-    pack(named, ranked, frac_ref[...], cell_ref[...], put)
-
-
-def pick_kernel(devices, owner_ref, count_ref, answer_ref, out_ref):
+    def put_ask(f, value):
+        ask_out[:, f, :] = value
+
+    pack(named, ranked, frac_ref[...], cell_ref[...], put_ask)
+    load.wait()
+    for x in range(cells_x):
+        stage[0, :, x : x + 1, :] = slabs[:, x + 1, cells_y - 1 :, :]
+        stage[1, :, x : x + 1, :] = slabs[:, x + 1, 0:1, :]
+        stage[2, :, x : x + 1, :] = slabs[:, x + 1, 1:2, :]
+    corner_out[...] = jnp.zeros(corner_out.shape, F32)
+    corner_out[0, :, 0:1, :] = slabs[:, 1, 0:1, :]
+    corner_out[0, :, 1:2, :] = slabs[:, 2, 0:1, :]
+    corner_out[0, :, 2:3, :] = slabs[:, 1, 1:2, :]
+    corner_out[1, :, 0:1, :] = slabs[:, cells_x, 0:1, :]
+    corner_out[2, :, 0:1, :] = slabs[:, 1, cells_y - 1 :, :]
+    ask_in[me] = ask_out[me]
+
+    pl.semaphore_wait(barrier, devices - 1)
+
+    def toward(order, source, target, dx, dy):
+        copy = pltpu.make_async_remote_copy(
+            src_ref=source,
+            dst_ref=target,
+            send_sem=near_send.at[order],
+            recv_sem=near_recv.at[order],
+            device_id={"gx": gx + dx, "gy": gy + dy},
+            device_id_type=pl.DeviceIdType.MESH,
+        )
+
+        def inside(sign):
+            ok = None
+            for place, count, by in ((gx, grid_x, sign * dx), (gy, grid_y, sign * dy)):
+                if by:
+                    one = place + by < count if by > 0 else place + by >= 0
+                    ok = one if ok is None else jnp.logical_and(ok, one)
+            return ok
+
+        return copy, inside(1), inside(-1)
+
+    tx, ty = tiles_x, tiles_y
+    field = [
+        (fv.at[:, cells_x - 1 : cells_x], slabs.at[:, 0:1], 1, 0),
+        (fv.at[:, 0:2], slabs.at[:, cells_x + 1 : cells_x + 3], -1, 0),
+        (stage.at[0], landed.at[0], 0, 1),
+        (stage.at[1:3], landed.at[1:3], 0, -1),
+        (corner_out.at[0], corner_in.at[0], -1, -1),
+        (corner_out.at[1], corner_in.at[1], 1, -1),
+        (corner_out.at[2], corner_in.at[2], -1, 1),
+    ]
+    particles = [
+        (packed.at[tx - 1], tiles.at[0, 1 : 1 + ty], 1, 0),
+        (packed.at[0], tiles.at[tx + 1, 1 : 1 + ty], -1, 0),
+        (packed.at[:, ty - 1], tiles.at[1 : 1 + tx, 0], 0, 1),
+        (packed.at[:, 0], tiles.at[1 : 1 + tx, ty + 1], 0, -1),
+        (packed.at[tx - 1, ty - 1], tiles.at[0, 0], 1, 1),
+        (packed.at[tx - 1, 0], tiles.at[0, ty + 1], 1, -1),
+        (packed.at[0, ty - 1], tiles.at[tx + 1, 0], -1, 1),
+        (packed.at[0, 0], tiles.at[tx + 1, ty + 1], -1, -1),
+    ]
+    copies = [toward(i, *one) for i, one in enumerate(field + particles)]
+
+    def exchange(out, into, send, recv, other, source):
+        return pltpu.make_async_remote_copy(
+            src_ref=out.at[other],
+            dst_ref=into.at[source],
+            send_sem=send.at[other],
+            recv_sem=recv.at[source],
+            device_id=at(other),
+            device_id_type=pl.DeviceIdType.MESH,
+        )
+
+    for copy, to, _ in copies[: len(field)]:
+        pl.when(to)(copy.start)
+    everyone(lambda other: exchange(ask_out, ask_in, ask_send, ask_recv, other, me).start())
+    for copy, to, _ in copies[len(field) :]:
+        pl.when(to)(copy.start)
+
+    def put_accel(m, n, result):
+        for d in range(3):
+            accel_out[d, m, pl.ds(n, 1), :] = result[d]
+
+    inner = tiles_y - 2
+    pair_forces(
+        tiles, put_accel, (tiles_x - 2) * inner, lambda i: (1 + i // inner, 1 + lax.rem(i, inner))
+    )
+
+    for copy, _, source in copies[: len(field)]:
+        pl.when(source)(copy.wait_recv)
+    y_low[:, 1 : 1 + cells_x] = landed[0]
+    y_up[:, 1 : 1 + cells_x] = landed[1]
+    y_up2[:, 1 : 1 + cells_x] = landed[2]
+    y_up[:, cells_x + 1 : cells_x + 3] = corner_in[0, :, 0:2]
+    y_up2[:, cells_x + 1 : cells_x + 2] = corner_in[0, :, 2:3]
+    y_up[:, 0:1] = corner_in[1, :, 0:1]
+    y_low[:, cells_x + 1 : cells_x + 2] = corner_in[2, :, 0:1]
+    keep_x = jnp.where(gx < grid_x - 1, 1.0, 0.0)
+    keep_y = jnp.where(gy < grid_y - 1, 1.0, 0.0)
+    sweep_block(slabs, y_low, y_up, y_up2, y_top, fresh, high, low, keep_x, keep_y)
+    store = pltpu.make_async_copy(fresh, fv_out, local_sem.at[1])
+    store.start()
+
+    everyone(lambda other: exchange(ask_out, ask_in, ask_send, ask_recv, me, other).wait_recv())
+    share = LANES // capacity
+    for q in range(devices // share):
+        total = ask_in[q * share]
+        for r in range(1, share):
+            total = total + pltpu.roll(ask_in[q * share + r], r * capacity, 1)
+        asked[:, q * LANES : (q + 1) * LANES] = total
+    width = 512
+
+    def put_reply(t, value):
+        for q in range(width // LANES):
+            part = value[:, q * LANES : (q + 1) * LANES]
+            for r in range(share):
+                turned = pltpu.roll(part, LANES - r * capacity, 1) if r else part
+                reply_out[t * (width // capacity) + q * share + r] = turned
+
+    interpolate(asked, high, low, fresh.shape, put_reply, width)
+    everyone(
+        lambda other: exchange(reply_out, reply_in, reply_send, reply_recv, other, me).start()
+    )
+    reply_in[me] = reply_out[me]
+
+    for copy, _, source in copies[len(field) :]:
+        pl.when(source)(copy.wait_recv)
+    pair_forces(
+        tiles, put_accel, 2 * ty, lambda i: ((i // ty) * (tiles_x - 1), lax.rem(i, ty))
+    )
+    pair_forces(
+        tiles,
+        put_accel,
+        2 * (tiles_x - 2),
+        lambda i: (1 + i // 2, lax.rem(i, 2) * (tiles_y - 1)),
+    )
+
+    everyone(
+        lambda other: exchange(
+            reply_out, reply_in, reply_send, reply_recv, me, other
+        ).wait_recv()
+    )
     named, ranked = route(owner_ref[...], count_ref[0], devices)
-    answers = jnp.concatenate([answer_ref[:, c, :] for c in range(4)], axis=0)
-    out_ref[...] = pick(named, ranked, answers)
-
-
-def block_kernel(slabs, y_low, y_up, y_up2, asked, fv_out, answer, high, low, y_top):
-    keep_x = jnp.where(lax.axis_index("gx") < lax.axis_size("gx") - 1, 1.0, 0.0)
-    keep_y = jnp.where(lax.axis_index("gy") < lax.axis_size("gy") - 1, 1.0, 0.0)
-    sweep_block(slabs, y_low, y_up, y_up2, y_top, fv_out, high, low, keep_x, keep_y)
-    width = 512
-
-    def put(t, value):
-        answer[:, pl.ds(pl.multiple_of(t * width, width), width)] = value
-
-    interpolate(asked, high, low, fv_out.shape, put, width)
-
-
-def sph_kernel(tiles_ref, out_ref):
-    tiles_x, tiles_y = out_ref.shape[1], out_ref.shape[2]
-
-    def put(m, n, result):
-        for d in range(3):
-            out_ref[d, m, pl.ds(n, 1), :] = result[d]
-
-    pair_forces(tiles_ref, put, tiles_x, tiles_y)
-
-
-def shifted(array, axis, by):
-    count = lax.axis_size(axis)
-    return lax.ppermute(array, axis, [(i, i + by) for i in range(count) if 0 <= i + by < count])
-
-
-PARAMS = pltpu.CompilerParams(vmem_limit_bytes=48 * 1024 * 1024)
-SMEM = pl.BlockSpec(memory_space=pltpu.SMEM)
-VMEM = pl.BlockSpec(memory_space=pltpu.VMEM)
+    answers = jnp.concatenate([reply_in[:, c, :] for c in range(4)], axis=0)
+    state_out[...] = pick(named, ranked, answers)
+
+    for copy, to, _ in copies:
+        pl.when(to)(copy.wait_send)
+    everyone(lambda other: exchange(ask_out, ask_in, ask_send, ask_recv, other, me).wait_send())
+    everyone(
+        lambda other: exchange(reply_out, reply_in, reply_send, reply_recv, other, me).wait_send()
+    )
+    store.wait()
 
 
 def per_device(
@@ -299,76 +483,67 @@
     sph_press,
     tile_count,
 ):
-    devices = lax.axis_size("gx") * lax.axis_size("gy")
+    grid = (lax.axis_size("gx"), lax.axis_size("gy"))
+    devices = grid[0] * grid[1]
     _, cells_x, cells_y, length = fv_state.shape
     rows = buffer_cell.shape[0]
     capacity = 2 * rows // devices
-    owner = buffer_owner.reshape(1, rows)
-    cell = buffer_cell.reshape(1, rows)
-    outgoing = pl.pallas_call(
-        functools.partial(pack_kernel, devices),
-        out_shape=jax.ShapeDtypeStruct((devices, 4, LANES), F32),
-        in_specs=[VMEM, VMEM, VMEM, SMEM],
-        out_specs=VMEM,
-        compiler_params=PARAMS,
-    )(owner, cell, buffer_frac, buffer_count)
-    arrived = lax.all_to_all(
-        outgoing[:, :, :capacity], ("gx", "gy"), split_axis=0, concat_axis=0, tiled=True
-    )
-    asked = jnp.transpose(arrived, (1, 0, 2)).reshape(4, devices * capacity)
-    before = shifted(fv_state[:, -1:], "gx", 1)
-    after = shifted(fv_state[:, :2], "gx", -1)
-    slabs = jnp.concatenate([before, fv_state, after], axis=1)
-    y_low = shifted(slabs[:, :, -1], "gy", 1)
-    y_up = shifted(slabs[:, :, :2], "gy", -1)
-    pad = ((0, 0), (0, 18 - cells_x - 3), (0, 0))
-    fv_next, answers = pl.pallas_call(
-        block_kernel,
-        out_shape=(
-            jax.ShapeDtypeStruct(fv_state.shape, F32),
-            jax.ShapeDtypeStruct((4, devices * capacity), F32),
-        ),
-        in_specs=[VMEM] * 5,
-        out_specs=(VMEM, VMEM),
-        scratch_shapes=[
-            pltpu.VMEM((4, (cells_x + 1) * cells_y + 16, length), BF16),
-            pltpu.VMEM((4, (cells_x + 1) * cells_y + 16, length), BF16),
-            pltpu.VMEM((4, 16, length), F32),
-        ],
-        compiler_params=PARAMS,
-    )(slabs, y_low, jnp.pad(y_up[:, :, 0], pad), jnp.pad(y_up[:, :, 1], pad), asked)
-    returned = lax.all_to_all(
-        jnp.transpose(answers.reshape(4, devices, capacity), (1, 0, 2)),
-        ("gx", "gy"),
-        split_axis=0,
-        concat_axis=0,
-        tiled=True,
-    )
-    buffer_state = pl.pallas_call(
-        functools.partial(pick_kernel, devices),
-        out_shape=jax.ShapeDtypeStruct((4, rows), F32),
-        in_specs=[VMEM, SMEM, VMEM],
-        out_specs=VMEM,
-        compiler_params=PARAMS,
-    )(owner, buffer_count, jnp.pad(returned, ((0, 0), (0, 0), (0, LANES - capacity))))
-    slots = sph_press.shape[2]
+    tiles_x, tiles_y, slots = sph_press.shape
     live = (jnp.arange(slots, dtype=jnp.int32) < tile_count[:, :, None]).astype(F32)
     packed = jnp.concatenate([sph_offset, sph_vel, sph_press[None], live[None]], axis=0)
     packed = jnp.transpose(packed, (1, 2, 0, 3))
-    packed = jnp.concatenate(
-        [shifted(packed[-1:], "gx", 1), packed, shifted(packed[:1], "gx", -1)], axis=0
-    )
-    packed = jnp.concatenate(
-        [shifted(packed[:, -1:], "gy", 1), packed, shifted(packed[:, :1], "gy", -1)], axis=1
-    )
-    sph_accel = pl.pallas_call(
-        sph_kernel,
-        out_shape=jax.ShapeDtypeStruct(sph_offset.shape, F32),
-        in_specs=[VMEM],
-        out_specs=VMEM,
-        compiler_params=PARAMS,
-    )(packed)
-    return fv_next, buffer_state, sph_accel
+    table = (cells_x + 1) * cells_y + 16
+    mail = pltpu.VMEM((devices, 4, LANES), F32)
+    dma = pltpu.SemaphoreType.DMA
+    vmem = pl.BlockSpec(memory_space=pltpu.VMEM)
+    anywhere = pl.BlockSpec(memory_space=pl.ANY)
+    return pl.pallas_call(
+        functools.partial(whole_kernel, grid, capacity),
+        out_shape=(
+            jax.ShapeDtypeStruct(fv_state.shape, F32),
+            jax.ShapeDtypeStruct((4, rows), F32),
+            jax.ShapeDtypeStruct(sph_offset.shape, F32),
+        ),
+        in_specs=[vmem, vmem, vmem, pl.BlockSpec(memory_space=pltpu.SMEM), anywhere, vmem],
+        out_specs=(anywhere, vmem, vmem),
+        scratch_shapes=[
+            pltpu.VMEM((4, cells_x + 3, cells_y, length), F32),
+            pltpu.VMEM((4, cells_x, cells_y, length), F32),
+            pltpu.VMEM((3, 4, cells_x, length), F32),
+            pltpu.VMEM((3, 4, cells_x, length), F32),
+            pltpu.VMEM((3, 4, 8, length), F32),
+            pltpu.VMEM((3, 4, 8, length), F32),
+            pltpu.VMEM((4, 24, length), F32),
+            pltpu.VMEM((4, 24, length), F32),
+            pltpu.VMEM((4, 24, length), F32),
+            pltpu.VMEM((4, 16, length), F32),
+            pltpu.VMEM((4, table, length), BF16),
+            pltpu.VMEM((4, table, length), BF16),
+            pltpu.VMEM((tiles_x + 2, tiles_y + 2, 8, slots), F32),
+            mail,
+            mail,
+            pltpu.VMEM((4, devices * capacity), F32),
+            mail,
+            mail,
+            dma((15,)),
+            dma((15,)),
+            dma((devices,)),
+            dma((devices,)),
+            dma((devices,)),
+            dma((devices,)),
+            dma((2,)),
+        ],
+        compiler_params=pltpu.CompilerParams(
+            collective_id=0, has_side_effects=True, vmem_limit_bytes=48 * 1024 * 1024
+        ),
+    )(
+        buffer_owner.reshape(1, rows),
+        buffer_cell.reshape(1, rows),
+        buffer_frac,
+        buffer_count,
+        fv_state,
+        packed,
+    )
 
 
 def solution(mesh):

time: 88.5 us -> 60.4 us (0.68)
  starting transfers between devices: 33.9 us -> 0 us
  Pallas kernels: 30.9 us -> 49.4 us
  waiting for transfers between devices: 7.99 us -> 0 us
  local copies, waits for them, and re-layouts: 10.7 us -> 7.72 us
  other arithmetic: 2.48 us -> 1.5 us
    ppermute x8 -> x0, starting transfers between devices: 21 us -> none  [shifted(): lax.ppermute(array, axis, [(i, i + by) for i in range(count) if 0 <= i +...]
    pallas_call x4 -> x1, Pallas kernels: 30.9 us -> 49.4 us  [per_device(): pl.pallas_call(functools.partial(whole_kernel, grid, capacity), out_shape...]
    all_to_all x2 -> x0, starting transfers between devices: 13 us -> none  [the longest x1 8 us: per_device(): lax.all_to_all(outgoing[:, :, :capacity], ('gx', 'gy'), split_axis=0, con...]
    ppermute x8 -> x0, waiting for transfers between devices: 5.49 us -> none  [shifted(): lax.ppermute(array, axis, [(i, i + by) for i in range(count) if 0 <= i +...]
    concatenate x1 -> x0, local copies, waits for them, and re-layouts: 3.86 us -> none  [per_device(): slabs = jnp.concatenate([before, fv_state, after], axis=1)]
    unnamed x23 -> x13, local copies, waits for them, and re-layouts: 4.53 us -> 7.72 us
    all_to_all x2 -> x0, waiting for transfers between devices: 2.49 us -> none  [the longest x1 2.49 us: per_device(): lax.all_to_all(outgoing[:, :, :capacity], ('gx', 'gy'), split_axis=0, con...]
    all_to_all x2 -> x0, other arithmetic: 1.44 us -> none  [the longest x1 0.72 us: per_device(): lax.all_to_all(jnp.transpose(answers.reshape(4, devices, capacity), (1, 0...]
  transfers between devices with their start and end apart: 10 -> 0, of which waited for: 3 -> 0; matrix products, arithmetic and copies ran while one was open for 11% -> 0% of each run, Pallas kernels for 34% -> 0%
where the time goes in v2:
time: 60.4 us; the launch traced here: 59.9 us
  Pallas kernels  49.4 us (82%)
  local copies, waits for them, and re-layouts  7.72 us (13%)
  other arithmetic  1.5 us (2%)
  between operations  1.31 us (2%)
    pallas_call x1, Pallas kernels, per_device(): pl.pallas_call(functools.partial(whole_kernel, grid, capacity), out_shape...  49.4 us
    unnamed x13, local copies, waits for them, and re-layouts  7.72 us

profile of v2, /device:TPU:1, one launch (start us, length us, event | category | flops | bytes accessed | tf_op | source)
XLA Modules:
  0.0 59.9 jit_solution(4355315747611948506)
XLA Ops:
  1.3 0.8 %compare_convert_fusion = f32[1,4,4,128]{3,0,2,1:T(1,128)S(1)} fusion(s32[4,4]{1,0:T(4,128)} %param.17), kind=kLoop, calls=%fused_computation.1 | loop fusion | flops 4096 | bytes 8256 | tf_op jit(solution)/shard_map/convert_element_type | solution.py:492
  2.0 0.8 %copy.12 = f32[3,4,4,128]{3,0,2,1:T(4,128)S(1)} copy(f32[3,4,4,128]{3,2,1,0:T(4,128)} %param.14) | data formatting | bytes 49152 | tf_op args[5]
  2.8 0.8 %copy.13 = f32[3,4,4,128]{3,0,2,1:T(4,128)S(1)} copy(f32[3,4,4,128]{3,2,1,0:T(4,128)} %param.15) | data formatting | bytes 49152 | tf_op args[6]
  3.6 0.7 %maximum_bitcast_fusion.packed = f32[4,4,8,128]{3,2,1,0:T(8,128)S(1)} fusion(f32[1,4,4,128]{3,0,2,1:T(1,128)S(1)} %compare_convert_fusion, f32[1,4,4,128]{3,0,2,1:T(1,128)} %bitcast.7, f32[3,4,4,128]{3,0,2,1:T(4,128)S(1)} %copy.13, f32[3,4,4,128]{3,0,2,1:T(4,128)S(1)} %copy.12), kind=kLoop, calls=%fused_computation | loop fusion | flops 49152 | bytes 131072 | tf_op jit(solution)/shard_map/transpose | solution.py:494
  4.3 0.0 copy-start
  4.3 1.6 %copy-done = f32[4,8,16,1024]{3,2,1,0:T(8,128)S(1)} copy-done((f32[4,8,16,1024]{3,2,1,0:T(8,128)S(1)}, f32[4,8,16,1024]{3,2,1,0:T(8,128)}, u32[]{:S(2)}) %copy-start) | copy-done | bytes 2097176
  5.9 0.0 copy-start.1
  5.9 0.7 %copy-done.1 = f32[3,1024]{1,0:T(4,128)S(1)} copy-done((f32[3,1024]{1,0:T(4,128)S(1)}, f32[3,1024]{1,0:T(4,128)}, u32[]{:S(2)}) %copy-start.1) | copy-done | bytes 12312
  6.6 0.0 copy-start.2
  6.6 0.7 %copy-done.2 = s32[1024,1]{0,1:T(1,128)S(1)} copy-done((s32[1024,1]{0,1:T(1,128)S(1)}, s32[1024,1]{0,1:T(1,128)}, u32[]{:S(2)}) %copy-start.2) | copy-done | bytes 4120
  7.3 0.0 copy-start.3
  7.3 0.7 %copy-done.3 = s32[1024]{0:T(1024)S(1)} copy-done((s32[1024]{0:T(1024)S(1)}, s32[1024]{0:T(1024)}, u32[]{:S(2)}) %copy-start.3) | copy-done | bytes 4120
  8.0 49.4 %shard_map.112 = (f32[4,8,16,1024]{3,2,1,0:T(8,128)S(1)}, f32[4,1024]{1,0:T(4,128)S(1)}, f32[3,4,4,128]{3,2,1,0:T(4,128)S(1)}) custom-call(s32[1,1024]{1,0:T(1,128)S(1)} %bitcast.5, s32[1,1024]{1,0:T(1,128)S(1)} %bitcast.6, f32[3,1024]{1,0:T(4,128)S(1)} %copy-done.1, s32[1]{0:T(128)S(6)} %copy.17.count_ref, f32[4,8,16,1024]{3,2,1,0:T(8,128)S(1)} %copy-done, ...), custom_call_target="tpu_custom_call" | custom-call | tf_op jit(solution)/shard_map/pallas_call | solution.py:500
  57.4 1.3 %copy.18 = f32[4,8,16,1024]{3,2,1,0:T(8,128)} copy(f32[4,8,16,1024]{3,2,1,0:T(8,128)S(1)} %get-tuple-element.6) | data formatting | bytes 4194304
  58.7 0.6 %copy.19 = f32[4,1024]{1,0:T(4,128)} copy(f32[4,1024]{1,0:T(4,128)S(1)} %get-tuple-element.7) | data formatting | bytes 32768
  59.3 0.6 %copy.20 = f32[3,4,4,128]{3,2,1,0:T(4,128)} copy(f32[3,4,4,128]{3,2,1,0:T(4,128)S(1)} %get-tuple-element.8) | data formatting | bytes 49152
Async XLA Ops:
  4.3 1.6 %copy-start = (f32[4,8,16,1024]{3,2,1,0:T(8,128)S(1)}, f32[4,8,16,1024]{3,2,1,0:T(8,128)}, u32[]{:S(2)}) copy-start(f32[4,8,16,1024]{3,2,1,0:T(8,128)} %fv.1) | copy-start | bytes 6291460
  5.9 0.7 %copy-start.1 = (f32[3,1024]{1,0:T(4,128)S(1)}, f32[3,1024]{1,0:T(4,128)}, u32[]{:S(2)}) copy-start(f32[3,1024]{1,0:T(4,128)} %frac_ref.1) | copy-start | bytes 36868
  6.6 0.7 %copy-start.2 = (s32[1024,1]{0,1:T(1,128)S(1)}, s32[1024,1]{0,1:T(1,128)}, u32[]{:S(2)}) copy-start(s32[1024,1]{0,1:T(1,128)} %param.10) | copy-start | bytes 12292
  7.3 0.7 %copy-start.3 = (s32[1024]{0:T(1024)S(1)}, s32[1024]{0:T(1024)}, u32[]{:S(2)}) copy-start(s32[1024]{0:T(1024)} %param.11) | copy-start | bytes 12292

commit v3 on v2

--- a/solution.py
+++ b/solution.py
@@ -203,16 +203,16 @@
     def one(index, carry):
         m, n = place(index)
         own = tiles[m + 1, n + 1]
-        sums = jnp.zeros((16, slots), F32)
+        column = jnp.transpose(own)
+        spread = [jnp.broadcast_to(column[:, d : d + 1], (slots, slots)) for d in range(3)]
+        w_high, w_low, f_high, f_low = [], [], [], []
         for a in range(3):
-            w_high, w_low, f_high, f_low = [], [], [], []
             for b in range(3):
-                other = tiles[m + a, n + b]
                 shift = jnp.where(row == 0, a - 1.0, jnp.where(row == 1, b - 1.0, 0.0))
-                other = other + shift
-                columns = jnp.transpose(other)
-                e = [own[d : d + 1] - columns[:, d : d + 1] for d in range(3)]
-                s = jnp.sqrt(e[0] * e[0] + e[1] * e[1] + e[2] * e[2])
+                other = tiles[m + a, n + b] + shift
+                e = [spread[d] - other[d : d + 1] for d in range(3)]
+                square = e[0] * e[0] + e[1] * e[1] + e[2] * e[2]
+                s = square * lax.rsqrt(jnp.maximum(square, 1e-30))
                 near = jnp.maximum(1.0 - s, 0.0)
                 high, low = split(near * near * near)
                 w_high.append(high)
@@ -221,10 +221,17 @@
                 high, low = split(jnp.concatenate([masked, masked * other[6:7]], axis=0))
                 f_high.append(high)
                 f_low.append(low)
-            w_high, w_low = jnp.concatenate(w_high, axis=0), jnp.concatenate(w_low, axis=0)
-            f_high, f_low = jnp.concatenate(f_high, axis=1), jnp.concatenate(f_low, axis=1)
-            both = dot(jnp.concatenate([f_high, f_low], axis=0), w_high)
-            sums = sums + both[:16] + both[16:] + dot(f_high, w_low)
+        weights = jnp.concatenate(
+            [jnp.concatenate(w_high, axis=1), jnp.concatenate(w_low, axis=1)], axis=0
+        )
+        factors = jnp.concatenate(
+            [jnp.concatenate(f_high, axis=1), jnp.concatenate(f_low, axis=1)], axis=0
+        )
+        both = lax.dot_general(
+            weights, factors, (((1,), (1,)), ((), ())), preferred_element_type=F32
+        )
+        both = jnp.transpose(both[:slots] + both[slots:])
+        sums = both[:16] + both[16:]
         result = []
         for d in range(3):
             push = (
@@ -248,7 +255,10 @@
     frac_ref,
     count_ref,
     fv,
-    packed,
+    offset_ref,
+    vel_ref,
+    press_ref,
+    tile_count_ref,
     fv_out,
     state_out,
     accel_out,
@@ -283,7 +293,7 @@
     gx, gy = lax.axis_index("gx"), lax.axis_index("gy")
     me = gx * grid_y + gy
     _, cells_x, cells_y, length = fresh.shape
-    tiles_x, tiles_y = packed.shape[0], packed.shape[1]
+    tiles_x, tiles_y, slots = press_ref.shape
     load = pltpu.make_async_copy(fv, slabs.at[:, 1 : 1 + cells_x], local_sem.at[0])
     load.start()
 
@@ -298,7 +308,13 @@
         tiles[m + 1, 0] = jnp.zeros(tiles.shape[2:], F32)
         tiles[m + 1, tiles_y + 1] = jnp.zeros(tiles.shape[2:], F32)
         for n in range(tiles_y):
-            tiles[m + 1, n + 1] = packed[m, n]
+            for d in range(3):
+                tiles[m + 1, n + 1, d : d + 1] = offset_ref[d, m, n : n + 1]
+                tiles[m + 1, n + 1, 3 + d : 4 + d] = vel_ref[d, m, n : n + 1]
+            tiles[m + 1, n + 1, 6:7] = press_ref[m, n : n + 1]
+            tiles[m + 1, n + 1, 7:8] = jnp.where(
+                lax.broadcasted_iota(jnp.int32, (1, slots), 1) < tile_count_ref[m, n], 1.0, 0.0
+            )
 
     def everyone(action):
         def step(p, carry):
@@ -369,14 +385,14 @@
         (corner_out.at[2], corner_in.at[2], -1, 1),
     ]
     particles = [
-        (packed.at[tx - 1], tiles.at[0, 1 : 1 + ty], 1, 0),
-        (packed.at[0], tiles.at[tx + 1, 1 : 1 + ty], -1, 0),
-        (packed.at[:, ty - 1], tiles.at[1 : 1 + tx, 0], 0, 1),
-        (packed.at[:, 0], tiles.at[1 : 1 + tx, ty + 1], 0, -1),
-        (packed.at[tx - 1, ty - 1], tiles.at[0, 0], 1, 1),
-        (packed.at[tx - 1, 0], tiles.at[0, ty + 1], 1, -1),
-        (packed.at[0, ty - 1], tiles.at[tx + 1, 0], -1, 1),
-        (packed.at[0, 0], tiles.at[tx + 1, ty + 1], -1, -1),
+        (tiles.at[tx, 1 : 1 + ty], tiles.at[0, 1 : 1 + ty], 1, 0),
+        (tiles.at[1, 1 : 1 + ty], tiles.at[tx + 1, 1 : 1 + ty], -1, 0),
+        (tiles.at[1 : 1 + tx, ty], tiles.at[1 : 1 + tx, 0], 0, 1),
+        (tiles.at[1 : 1 + tx, 1], tiles.at[1 : 1 + tx, ty + 1], 0, -1),
+        (tiles.at[tx, ty], tiles.at[0, 0], 1, 1),
+        (tiles.at[tx, 1], tiles.at[0, ty + 1], 1, -1),
+        (tiles.at[1, ty], tiles.at[tx + 1, 0], -1, 1),
+        (tiles.at[1, 1], tiles.at[tx + 1, ty + 1], -1, -1),
     ]
     copies = [toward(i, *one) for i, one in enumerate(field + particles)]
 
@@ -403,6 +419,15 @@
     inner = tiles_y - 2
     pair_forces(
         tiles, put_accel, (tiles_x - 2) * inner, lambda i: (1 + i // inner, 1 + lax.rem(i, inner))
+    )
+
+    for copy, _, source in copies[len(field) :]:
+        pl.when(source)(copy.wait_recv)
+    pair_forces(
+        tiles,
+        put_accel,
+        2 * (tiles_x - 2),
+        lambda i: (1 + i // 2, lax.rem(i, 2) * (tiles_y - 1)),
     )
 
     for copy, _, source in copies[: len(field)]:
@@ -442,16 +467,8 @@
     )
     reply_in[me] = reply_out[me]
 
-    for copy, _, source in copies[len(field) :]:
-        pl.when(source)(copy.wait_recv)
     pair_forces(
         tiles, put_accel, 2 * ty, lambda i: ((i // ty) * (tiles_x - 1), lax.rem(i, ty))
-    )
-    pair_forces(
-        tiles,
-        put_accel,
-        2 * (tiles_x - 2),
-        lambda i: (1 + i // 2, lax.rem(i, 2) * (tiles_y - 1)),
     )
 
     everyone(
@@ -489,13 +506,11 @@
     rows = buffer_cell.shape[0]
     capacity = 2 * rows // devices
     tiles_x, tiles_y, slots = sph_press.shape
-    live = (jnp.arange(slots, dtype=jnp.int32) < tile_count[:, :, None]).astype(F32)
-    packed = jnp.concatenate([sph_offset, sph_vel, sph_press[None], live[None]], axis=0)
-    packed = jnp.transpose(packed, (1, 2, 0, 3))
     table = (cells_x + 1) * cells_y + 16
     mail = pltpu.VMEM((devices, 4, LANES), F32)
     dma = pltpu.SemaphoreType.DMA
     vmem = pl.BlockSpec(memory_space=pltpu.VMEM)
+    scalars = pl.BlockSpec(memory_space=pltpu.SMEM)
     anywhere = pl.BlockSpec(memory_space=pl.ANY)
     return pl.pallas_call(
         functools.partial(whole_kernel, grid, capacity),
@@ -504,7 +519,7 @@
             jax.ShapeDtypeStruct((4, rows), F32),
             jax.ShapeDtypeStruct(sph_offset.shape, F32),
         ),
-        in_specs=[vmem, vmem, vmem, pl.BlockSpec(memory_space=pltpu.SMEM), anywhere, vmem],
+        in_specs=[vmem, vmem, vmem, scalars, anywhere, vmem, vmem, vmem, scalars],
         out_specs=(anywhere, vmem, vmem),
         scratch_shapes=[
             pltpu.VMEM((4, cells_x + 3, cells_y, length), F32),
@@ -534,7 +549,7 @@
             dma((2,)),
         ],
         compiler_params=pltpu.CompilerParams(
-            collective_id=0, has_side_effects=True, vmem_limit_bytes=48 * 1024 * 1024
+            collective_id=0, has_side_effects=True, vmem_limit_bytes=62 * 1024 * 1024
         ),
     )(
         buffer_owner.reshape(1, rows),
@@ -542,7 +557,10 @@
         buffer_frac,
         buffer_count,
         fv_state,
-        packed,
+        sph_offset,
+        sph_vel,
+        sph_press,
+        tile_count,
     )
 
 

time: 60.4 us -> 53.7 us (0.89)
  local copies, waits for them, and re-layouts: 7.72 us -> 4.39 us
  Pallas kernels: 49.4 us -> 47.8 us
  other arithmetic: 1.5 us -> 0 us
    unnamed x13 -> x7, local copies, waits for them, and re-layouts: 7.72 us -> 4.39 us
    pallas_call x1, Pallas kernels: 49.4 us -> 47.8 us  [per_device(): pl.pallas_call(functools.partial(whole_kernel, grid, capacity), out_shape...]
    convert_element_type x1 -> x0, other arithmetic: 0.76 us -> none  [per_device(): (jnp.arange(slots, dtype=jnp.int32) < tile_count[:, :, None]).astype(F32)]
    transpose x1 -> x0, other arithmetic: 0.73 us -> none  [per_device(): packed = jnp.transpose(packed, (1, 2, 0, 3))]
where the time goes in v3:
time: 53.7 us; the launch traced here: 53.5 us
  Pallas kernels  47.8 us (89%)
  local copies, waits for them, and re-layouts  4.39 us (8%)
  between operations  1.3 us (2%)
    pallas_call x1, Pallas kernels, per_device(): pl.pallas_call(functools.partial(whole_kernel, grid, capacity), out_shape...  47.8 us
    unnamed x7, local copies, waits for them, and re-layouts  4.39 us

profile of v3, /device:TPU:1, one launch (start us, length us, event | category | flops | bytes accessed | tf_op | source)
XLA Modules:
  0.0 53.5 jit_solution(11034393305086316651)
XLA Ops:
  1.3 47.8 %shard_map.112 = (f32[4,8,16,1024]{3,2,1,0:T(8,128)}, f32[4,1024]{1,0:T(4,128)}, f32[3,4,4,128]{3,2,1,0:T(4,128)}) custom-call(s32[1,1024]{1,0:T(1,128)} %bitcast.2, s32[1,1024]{1,0:T(1,128)} %bitcast.3, f32[3,1024]{1,0:T(4,128)} %frac_ref.1, s32[1]{0:T(128)S(6)} %copy.15.count_ref, f32[4,8,16,1024]{3,2,1,0:T(8,128)} %fv.1, f32[3,4,4,128]{3,2,1,0:T(4,128)} %offset_ref.1, ...), custom_call_target="tpu_custom_call" | custom-call | tf_op jit(solution)/shard_map/pallas_call | solution.py:515
  49.0 0.0 copy-start.1
  49.1 0.0 copy-start
  49.1 3.2 %copy.16 = f32[4,8,16,1024]{3,2,1,0:T(8,128)} copy(f32[4,8,16,1024]{3,2,1,0:T(8,128)} %get-tuple-element.6) | data formatting | bytes 4194304
  52.2 0.0 copy-done.1
  52.2 0.6 %copy.17 = f32[4,1024]{1,0:T(4,128)} copy(f32[4,1024]{1,0:T(4,128)S(1)} %copy-done.1) | data formatting | bytes 32768
  52.8 0.0 copy-done
  52.9 0.6 %copy.18 = f32[3,4,4,128]{3,2,1,0:T(4,128)} copy(f32[3,4,4,128]{3,2,1,0:T(4,128)S(1)} %copy-done) | data formatting | bytes 49152
Async XLA Ops:
  49.0 3.2 %copy-start.1 = (f32[4,1024]{1,0:T(4,128)S(1)}, f32[4,1024]{1,0:T(4,128)}, u32[]{:S(2)}) copy-start(f32[4,1024]{1,0:T(4,128)} %get-tuple-element.7) | copy-start | bytes 49156
  49.1 3.8 %copy-start = (f32[3,4,4,128]{3,2,1,0:T(4,128)S(1)}, f32[3,4,4,128]{3,2,1,0:T(4,128)}, u32[]{:S(2)}) copy-start(f32[3,4,4,128]{3,2,1,0:T(4,128)} %get-tuple-element.8) | copy-start | bytes 73732

commit v4 on v3

--- a/solution.py
+++ b/solution.py
@@ -339,17 +339,6 @@
         ask_out[:, f, :] = value
 
     pack(named, ranked, frac_ref[...], cell_ref[...], put_ask)
-    load.wait()
-    for x in range(cells_x):
-        stage[0, :, x : x + 1, :] = slabs[:, x + 1, cells_y - 1 :, :]
-        stage[1, :, x : x + 1, :] = slabs[:, x + 1, 0:1, :]
-        stage[2, :, x : x + 1, :] = slabs[:, x + 1, 1:2, :]
-    corner_out[...] = jnp.zeros(corner_out.shape, F32)
-    corner_out[0, :, 0:1, :] = slabs[:, 1, 0:1, :]
-    corner_out[0, :, 1:2, :] = slabs[:, 2, 0:1, :]
-    corner_out[0, :, 2:3, :] = slabs[:, 1, 1:2, :]
-    corner_out[1, :, 0:1, :] = slabs[:, cells_x, 0:1, :]
-    corner_out[2, :, 0:1, :] = slabs[:, 1, cells_y - 1 :, :]
     ask_in[me] = ask_out[me]
 
     pl.semaphore_wait(barrier, devices - 1)
@@ -406,11 +395,24 @@
             device_id_type=pl.DeviceIdType.MESH,
         )
 
-    for copy, to, _ in copies[: len(field)]:
+    for copy, to, _ in copies[len(field) :]:
+        pl.when(to)(copy.start)
+    for copy, to, _ in copies[:2]:
+        pl.when(to)(copy.start)
+    load.wait()
+    for x in range(cells_x):
+        stage[0, :, x : x + 1, :] = slabs[:, x + 1, cells_y - 1 :, :]
+        stage[1, :, x : x + 1, :] = slabs[:, x + 1, 0:1, :]
+        stage[2, :, x : x + 1, :] = slabs[:, x + 1, 1:2, :]
+    corner_out[...] = jnp.zeros(corner_out.shape, F32)
+    corner_out[0, :, 0:1, :] = slabs[:, 1, 0:1, :]
+    corner_out[0, :, 1:2, :] = slabs[:, 2, 0:1, :]
+    corner_out[0, :, 2:3, :] = slabs[:, 1, 1:2, :]
+    corner_out[1, :, 0:1, :] = slabs[:, cells_x, 0:1, :]
+    corner_out[2, :, 0:1, :] = slabs[:, 1, cells_y - 1 :, :]
+    for copy, to, _ in copies[2 : len(field)]:
         pl.when(to)(copy.start)
     everyone(lambda other: exchange(ask_out, ask_in, ask_send, ask_recv, other, me).start())
-    for copy, to, _ in copies[len(field) :]:
-        pl.when(to)(copy.start)
 
     def put_accel(m, n, result):
         for d in range(3):
@@ -476,7 +478,6 @@
             reply_out, reply_in, reply_send, reply_recv, me, other
         ).wait_recv()
     )
-    named, ranked = route(owner_ref[...], count_ref[0], devices)
     answers = jnp.concatenate([reply_in[:, c, :] for c in range(4)], axis=0)
     state_out[...] = pick(named, ranked, answers)
 
@@ -519,15 +520,15 @@
             jax.ShapeDtypeStruct((4, rows), F32),
             jax.ShapeDtypeStruct(sph_offset.shape, F32),
         ),
-        in_specs=[vmem, vmem, vmem, scalars, anywhere, vmem, vmem, vmem, scalars],
+        in_specs=[vmem, vmem, vmem, scalars, pl.BlockSpec(memory_space=pltpu.HBM), vmem, vmem, vmem, scalars],
         out_specs=(anywhere, vmem, vmem),
         scratch_shapes=[
             pltpu.VMEM((4, cells_x + 3, cells_y, length), F32),
             pltpu.VMEM((4, cells_x, cells_y, length), F32),
             pltpu.VMEM((3, 4, cells_x, length), F32),
             pltpu.VMEM((3, 4, cells_x, length), F32),
-            pltpu.VMEM((3, 4, 8, length), F32),
-            pltpu.VMEM((3, 4, 8, length), F32),
+            pltpu.VMEM((3, 4, 4, length), F32),
+            pltpu.VMEM((3, 4, 4, length), F32),
             pltpu.VMEM((4, 24, length), F32),
             pltpu.VMEM((4, 24, length), F32),
             pltpu.VMEM((4, 24, length), F32),

time: 53.7 us -> 49 us (0.912)
  Pallas kernels: 47.8 us -> 43.1 us
    pallas_call x1, Pallas kernels: 47.8 us -> 43.1 us  [per_device(): pl.pallas_call(functools.partial(whole_kernel, grid, capacity), out_shape...]
where the time goes in v4:
time: 49 us; the launch traced here: 48.8 us
  Pallas kernels  43.1 us (88%)
  local copies, waits for them, and re-layouts  4.39 us (9%)
  between operations  1.3 us (3%)
    pallas_call x1, Pallas kernels, per_device(): pl.pallas_call(functools.partial(whole_kernel, grid, capacity), out_shape...  43.1 us
    unnamed x7, local copies, waits for them, and re-layouts  4.39 us

profile of v4, /device:TPU:1, one launch (start us, length us, event | category | flops | bytes accessed | tf_op | source)
XLA Modules:
  0.0 48.8 jit_solution(11392131973074365105)
XLA Ops:
  1.3 43.1 %shard_map.112 = (f32[4,8,16,1024]{3,2,1,0:T(8,128)}, f32[4,1024]{1,0:T(4,128)}, f32[3,4,4,128]{3,2,1,0:T(4,128)}) custom-call(s32[1,1024]{1,0:T(1,128)} %bitcast.2, s32[1,1024]{1,0:T(1,128)} %bitcast.3, f32[3,1024]{1,0:T(4,128)} %frac_ref.1, s32[1]{0:T(128)S(6)} %copy.15.count_ref, f32[4,8,16,1024]{3,2,1,0:T(8,128)} %fv.1, f32[3,4,4,128]{3,2,1,0:T(4,128)} %offset_ref.1, ...), custom_call_target="tpu_custom_call" | custom-call | tf_op jit(solution)/shard_map/pallas_call | solution.py:516
  44.4 0.0 copy-start.1
  44.4 0.0 copy-start
  44.4 3.2 %copy.16 = f32[4,8,16,1024]{3,2,1,0:T(8,128)} copy(f32[4,8,16,1024]{3,2,1,0:T(8,128)} %get-tuple-element.6) | data formatting | bytes 4194304
  47.6 0.0 copy-done.1
  47.6 0.6 %copy.17 = f32[4,1024]{1,0:T(4,128)} copy(f32[4,1024]{1,0:T(4,128)S(1)} %copy-done.1) | data formatting | bytes 32768
  48.2 0.0 copy-done
  48.2 0.6 %copy.18 = f32[3,4,4,128]{3,2,1,0:T(4,128)} copy(f32[3,4,4,128]{3,2,1,0:T(4,128)S(1)} %copy-done) | data formatting | bytes 49152
Async XLA Ops:
  44.4 3.2 %copy-start.1 = (f32[4,1024]{1,0:T(4,128)S(1)}, f32[4,1024]{1,0:T(4,128)}, u32[]{:S(2)}) copy-start(f32[4,1024]{1,0:T(4,128)} %get-tuple-element.7) | copy-start | bytes 49156
  44.4 3.8 %copy-start = (f32[3,4,4,128]{3,2,1,0:T(4,128)S(1)}, f32[3,4,4,128]{3,2,1,0:T(4,128)}, u32[]{:S(2)}) copy-start(f32[3,4,4,128]{3,2,1,0:T(4,128)} %get-tuple-element.8) | copy-start | bytes 73732
